TPU v7x, 32 devices: a whole 2x2x4 slice. The times are simulated.
32 devices in a mesh: batch: 16 (over z, y, x), tp: 2 (over core).
Axes of the slice: x: 2, y: 2, z: 4, core: 2. Of those that a mesh axis runs over, the one named last changes fastest.
Arguments:
- tokens: bfloat16 [19456, 768], P('batch'), may hold values from -6 to 6
- seq_ids: int32 [19456], P('batch'), may hold values from 0 to 5, as said below
- cotangent: bfloat16 [19456, 768], P('batch'), may hold values from -6 to 6
- norm1_gain: float32 [768], replicated, may hold values from 0.1 to 1.9
- norm1_shift: float32 [768], replicated, may hold values from -3 to 3
- w_qkv: bfloat16 [768, 3, 768], P(None, None, 'tp'), may hold values from -0.21875 to 0.21875
- qv_bias: float32 [2, 768], P(None, 'tp'), may hold values from -3 to 3
- w_out: bfloat16 [768, 768], P('tp'), may hold values from -1.75 to 1.75
- out_bias: float32 [768], replicated, may hold values from -3 to 3
- norm2_gain: float32 [768], replicated, may hold values from 0.1 to 1.9
- norm2_shift: float32 [768], replicated, may hold values from -3 to 3
- w_in: bfloat16 [768, 3072], P(None, 'tp'), may hold values from -0.21875 to 0.21875
- in_bias: float32 [3072], P('tp'), may hold values from -3 to 3
- w_back: bfloat16 [3072, 768], P('tp'), may hold values from -0.109375 to 0.109375
- back_bias: float32 [768], replicated, may hold values from -3 to 3
Outputs:
- layer_out: bfloat16 [19456, 768], P('batch')
- tokens_grad: bfloat16 [19456, 768], P('batch')
- norm1_gain_grad: float32 [768], P('batch')
- norm1_shift_grad: float32 [768], P('batch')
- w_qkv_grad: float32 [768, 3, 768], P('batch', None, 'tp')
- qv_bias_grad: float32 [2, 768], P(None, ('tp', 'batch'))
- w_out_grad: float32 [768, 768], P('tp', 'batch')
- out_bias_grad: float32 [768], P('batch')
- norm2_gain_grad: float32 [768], P('batch')
- norm2_shift_grad: float32 [768], P('batch')
- w_in_grad: float32 [768, 3072], P('batch', 'tp')
- in_bias_grad: float32 [3072], P(('tp', 'batch'))
- w_back_grad: float32 [3072, 768], P('tp', 'batch')
- back_bias_grad: float32 [768], P('batch')
Inputs may be any that keep to these rules, and one draw needn't show every extreme that they name: `seq_ids`: in each aligned block of 1216 tokens, ids start at 0 and never fall; sequences of 608 tokens come first, then sequences of 228; the last may be cut by the block's end; some block holds only sequences of 228.
All inputs are finite; a program needn't handle non-finite values.
Results may differ from a plain program's by a relative error of at most 0.012.
Values sent between devices are 32-bit elements; how exact they have to be, the bound alone decides.
A program may use at most 192 MiB of HBM per device.

v0:
```python
import jax
import jax.numpy as jnp
from jax import lax
from jax.sharding import PartitionSpec as P

HEAD_DIM = 64
QBLOCK = 608


def normalize(values, norm_gain, norm_shift):
    center = values - jnp.mean(values, -1, keepdims=True)
    spread = jnp.mean(center * center, -1, keepdims=True)
    return center * lax.rsqrt(spread + 1e-06) * norm_gain + norm_shift


def masked_scores(rows, row_ids, keys, segment):
    scores = jnp.einsum(
        "qhe,khe->hqk", rows, keys, preferred_element_type=jnp.float32
    ) * HEAD_DIM ** (-0.5)
    allowed = (row_ids[:, None] == segment[None, :])[None]
    return jnp.where(allowed, scores, -1000000000.0)


def attend_forward(query, keys, values, segment):
    tok_count, head_count, width = query.shape
    count = tok_count // QBLOCK
    blocks = (query.reshape(count, QBLOCK, head_count, width), segment.reshape(count, QBLOCK))

    def one_block(item):
        rows, row_ids = item
        scores = masked_scores(rows, row_ids, keys, segment)
        top = jnp.max(scores, -1, keepdims=True)
        expo = jnp.exp(scores - top)
        total = jnp.sum(expo, -1, keepdims=True)
        weights = (expo / total).astype(jnp.bfloat16)
        mixed = jnp.einsum("hqk,khe->qhe", weights, values, preferred_element_type=jnp.float32)
        return (mixed, (top + jnp.log(total))[:, :, 0])

    mixed, log_total = lax.map(one_block, blocks)
    return (mixed.reshape(tok_count, head_count * width).astype(jnp.bfloat16), log_total)


def attend_backward(query, keys, values, segment, log_total, grad_mixed):
    tok_count, head_count, width = query.shape
    count = tok_count // QBLOCK
    scale = HEAD_DIM ** (-0.5)
    blocks = (
        query.reshape(count, QBLOCK, head_count, width),
        segment.reshape(count, QBLOCK),
        log_total,
        grad_mixed.reshape(count, QBLOCK, head_count, width),
    )

    def one_block(carry, item):
        grad_keys, grad_values = carry
        rows, row_ids, lse_rows, grad_rows = item
        scores = masked_scores(rows, row_ids, keys, segment)
        probs = jnp.exp(scores - lse_rows[:, :, None])
        grad_probs = jnp.einsum(
            "qhe,khe->hqk", grad_rows, values, preferred_element_type=jnp.float32
        )
        inner = jnp.sum(probs * grad_probs, -1, keepdims=True)
        grad_scores = (probs * (grad_probs - inner)).astype(jnp.bfloat16)
        grad_query = (
            jnp.einsum("hqk,khe->qhe", grad_scores, keys, preferred_element_type=jnp.float32)
            * scale
        )
        grad_keys = (
            grad_keys
            + jnp.einsum("hqk,qhe->khe", grad_scores, rows, preferred_element_type=jnp.float32)
            * scale
        )
        grad_values = grad_values + jnp.einsum(
            "hqk,qhe->khe",
            probs.astype(jnp.bfloat16),
            grad_rows,
            preferred_element_type=jnp.float32,
        )
        return ((grad_keys, grad_values), grad_query)

    zeros = jnp.zeros(keys.shape, jnp.float32)
    (grad_keys, grad_values), grad_query = lax.scan(one_block, (zeros, zeros), blocks)
    return (
        grad_query.reshape(tok_count, head_count * width),
        grad_keys.reshape(tok_count, head_count * width),
        grad_values.reshape(tok_count, head_count * width),
    )


def attention_front(inputs, segment, norm1_gain, norm1_shift, w_qkv, qv_bias, w_out):
    tok_count = inputs.shape[0]
    head_count = w_qkv.shape[2] // HEAD_DIM
    normed = normalize(inputs, norm1_gain, norm1_shift).astype(jnp.bfloat16)
    proj = jnp.einsum("td,dcf->tcf", normed, w_qkv, preferred_element_type=jnp.float32)
    query = (proj[:, 0] + qv_bias[0]).astype(jnp.bfloat16).reshape(tok_count, head_count, HEAD_DIM)
    keys = proj[:, 1].astype(jnp.bfloat16).reshape(tok_count, head_count, HEAD_DIM)
    values = (proj[:, 2] + qv_bias[1]).astype(jnp.bfloat16).reshape(tok_count, head_count, HEAD_DIM)
    mixed, log_total = attend_forward(query, keys, values, segment)
    partial_out = jnp.dot(mixed, w_out, preferred_element_type=jnp.float32)
    return (normed, query, keys, values, mixed, log_total, partial_out)


def mlp_front(inputs, summed, out_bias, norm2_gain, norm2_shift, w_in, in_bias):
    middle = inputs + summed + out_bias
    normed_two = normalize(middle, norm2_gain, norm2_shift).astype(jnp.bfloat16)
    hidden_pre = jnp.dot(normed_two, w_in, preferred_element_type=jnp.float32) + in_bias
    return (middle, normed_two, hidden_pre)


def shards(
    tokens,
    seq_ids,
    cotangent,
    norm1_gain,
    norm1_shift,
    w_qkv,
    qv_bias,
    w_out,
    out_bias,
    norm2_gain,
    norm2_shift,
    w_in,
    in_bias,
    w_back,
    back_bias,
):
    inputs = tokens.astype(jnp.float32)
    normed, query, keys, values, mixed, log_total, partial_out = attention_front(
        inputs, seq_ids, norm1_gain, norm1_shift, w_qkv, qv_bias, w_out
    )
    summed = lax.psum(partial_out, "tp")
    middle, normed_two, hidden_pre = mlp_front(
        inputs, summed, out_bias, norm2_gain, norm2_shift, w_in, in_bias
    )
    hidden = jax.nn.gelu(hidden_pre).astype(jnp.bfloat16)
    mlp_partial = jnp.dot(hidden, w_back, preferred_element_type=jnp.float32)
    mlp_out = lax.psum(mlp_partial, "tp")
    layer_out = (middle + mlp_out + back_bias).astype(jnp.bfloat16)
    fenced = lax.optimization_barrier(
        (
            layer_out,
            inputs,
            seq_ids,
            norm1_gain,
            norm1_shift,
            w_qkv,
            qv_bias,
            w_out,
            out_bias,
            norm2_gain,
            norm2_shift,
            w_in,
            in_bias,
        )
    )
    layer_out = fenced[0]
    normed, query, keys, values, mixed, log_total, partial_out = attention_front(
        fenced[1], fenced[2], fenced[3], fenced[4], fenced[5], fenced[6], fenced[7]
    )
    summed = lax.psum(partial_out, "tp")
    middle, normed_two, hidden_pre = mlp_front(
        fenced[1], summed, fenced[8], fenced[9], fenced[10], fenced[11], fenced[12]
    )
    hidden = jax.nn.gelu(hidden_pre).astype(jnp.bfloat16)
    grad_out = cotangent.astype(jnp.float32)
    back_bias_grad = jnp.sum(grad_out, 0)
    w_back_grad = jnp.einsum("tf,td->fd", hidden, cotangent, preferred_element_type=jnp.float32)
    grad_hidden = jnp.einsum("td,fd->tf", cotangent, w_back, preferred_element_type=jnp.float32)
    gelu_pull = jax.vjp(jax.nn.gelu, hidden_pre)[1]
    grad_pre = gelu_pull(grad_hidden)[0].astype(jnp.bfloat16)
    in_bias_grad = jnp.sum(grad_pre.astype(jnp.float32), 0)
    w_in_grad = jnp.einsum("td,tf->df", normed_two, grad_pre, preferred_element_type=jnp.float32)
    grad_normed_two = lax.psum(
        jnp.einsum("tf,df->td", grad_pre, w_in, preferred_element_type=jnp.float32), "tp"
    )
    norm2_pull = jax.vjp(normalize, middle, norm2_gain, norm2_shift)[1]
    grad_middle_add, norm2_gain_grad, norm2_shift_grad = norm2_pull(grad_normed_two)
    grad_middle = grad_out + grad_middle_add
    mlp_vectors = jnp.stack([norm2_gain_grad, norm2_shift_grad, back_bias_grad])
    grad_branch = grad_middle.astype(jnp.bfloat16)
    out_bias_grad = jnp.sum(grad_branch.astype(jnp.float32), 0)
    w_out_grad = jnp.einsum("tf,td->fd", mixed, grad_branch, preferred_element_type=jnp.float32)
    grad_mixed = jnp.einsum(
        "td,fd->tf", grad_branch, w_out, preferred_element_type=jnp.float32
    ).astype(jnp.bfloat16)
    grad_query, grad_keys, grad_values = attend_backward(
        query, keys, values, seq_ids, log_total, grad_mixed
    )
    grad_proj = jnp.stack([grad_query, grad_keys, grad_values], 1).astype(jnp.bfloat16)
    grad_wide = grad_proj.astype(jnp.float32)
    qv_bias_grad = jnp.stack([jnp.sum(grad_wide[:, 0], 0), jnp.sum(grad_wide[:, 2], 0)])
    w_qkv_grad = jnp.einsum("td,tcf->dcf", normed, grad_proj, preferred_element_type=jnp.float32)
    grad_normed = lax.psum(
        jnp.einsum("tcf,dcf->td", grad_proj, w_qkv, preferred_element_type=jnp.float32), "tp"
    )
    norm1_pull = jax.vjp(normalize, inputs, norm1_gain, norm1_shift)[1]
    grad_input_add, norm1_gain_grad, norm1_shift_grad = norm1_pull(grad_normed)
    tokens_grad = (grad_middle + grad_input_add).astype(jnp.bfloat16)
    attn_vectors = jnp.stack([norm1_gain_grad, norm1_shift_grad, out_bias_grad])
    w_qkv_part, qv_bias_part, w_out_part, w_in_part, in_bias_part, w_back_part, all_vectors = (
        lax.psum_scatter(w_qkv_grad, "batch", scatter_dimension=0, tiled=True),
        lax.psum_scatter(qv_bias_grad, "batch", scatter_dimension=1, tiled=True),
        lax.psum_scatter(w_out_grad, "batch", scatter_dimension=1, tiled=True),
        lax.psum_scatter(w_in_grad, "batch", scatter_dimension=0, tiled=True),
        lax.psum_scatter(in_bias_grad, "batch", scatter_dimension=0, tiled=True),
        lax.psum_scatter(w_back_grad, "batch", scatter_dimension=1, tiled=True),
        lax.psum_scatter(
            jnp.concatenate([attn_vectors, mlp_vectors], 0),
            "batch",
            scatter_dimension=1,
            tiled=True,
        ),
    )
    attn_vector_part = all_vectors[0:3]
    mlp_vector_part = all_vectors[3:6]
    return (
        layer_out,
        tokens_grad,
        attn_vector_part[0],
        attn_vector_part[1],
        w_qkv_part,
        qv_bias_part,
        w_out_part,
        attn_vector_part[2],
        mlp_vector_part[0],
        mlp_vector_part[1],
        w_in_part,
        in_bias_part,
        w_back_part,
        mlp_vector_part[2],
    )


def solution(mesh):
    in_specs = (
        P("batch", None),
        P("batch"),
        P("batch", None),
        P(),
        P(),
        P(None, None, "tp"),
        P(None, "tp"),
        P("tp", None),
        P(),
        P(),
        P(),
        P(None, "tp"),
        P("tp"),
        P("tp", None),
        P(),
    )
    out_specs = (
        P("batch", None),
        P("batch", None),
        P("batch"),
        P("batch"),
        P("batch", None, "tp"),
        P(None, ("tp", "batch")),
        P("tp", "batch"),
        P("batch"),
        P("batch"),
        P("batch"),
        P("batch", "tp"),
        P(("tp", "batch")),
        P("tp", "batch"),
        P("batch"),
    )
    return jax.shard_map(shards, mesh=mesh, in_specs=in_specs, out_specs=out_specs, check_vma=False)
```

profile of v0, /device:TPU:0, one launch (start us, length us, event | category | flops | bytes accessed | tf_op | source)
XLA Modules:
  0.0 1212.7 jit_solution(3598641540872090022)
XLA Ops:
  34.3 38.7 %while.37 = (s32[]{:T(128)}, bf16[2,608,6,64]{1,3,2,0:T(8,128)(2,1)}, s32[2,608]{1,0:T(2,128)S(1)}, s32[1216]{0:T(1024)S(1)}, bf16[2,608,6,64]{1,3,2,0:T(8,128)(...) while((s32[]{:T(128)}, bf16[2,608,6,64]{1,3,2,0:T(8,128)(2,1)}, ...), condition=%wide.region_5.6_spmd, body=%wide.region_2.5_spmd.sunk | while | flops 1744080896 | bytes 7126501 | solution.py:39
  43.0 10.6 fusion.193
  62.1 10.6 fusion.193
  83.5 27.1 %all-reduce.9.cloned.1.call-done = f32[1216,768]{1,0:T(8,128)} async-done(((f32[1216,768]{1,0:T(8,128)}), f32[1216,768]{1,0:T(8,128)}) %all-reduce.9.cloned.1.call-update) | async-done | bytes 3735568 | tf_op jit(solution)/shard_map/psum | solution.py:131
  115.9 10.8 fusion.99
  130.4 22.0 %all-reduce.11.cloned.1.call-done = f32[1216,768]{1,0:T(8,128)} async-done(((f32[1216,768]{1,0:T(8,128)}), f32[1216,768]{1,0:T(8,128)}) %all-reduce.11.cloned.1.call-update) | async-done | bytes 3735568 | tf_op jit(solution)/shard_map/psum | solution.py:137
  188.3 56.3 %while.38 = (s32[]{:T(128)}, bf16[2,608,6,64]{1,3,2,0:T(8,128)(2,1)}, f32[2,6,608]{2,1,0:T(8,128)S(1)}, s32[2,608]{1,0:T(2,128)S(1)}, s32[1216]{0:T(1024)S(1)}, ...) while((s32[]{:T(128)}, ...), condition=%wide.region_15.16_spmd, body=%wide.region_12.15_spmd.sunk | while | flops 1171831296 | bytes 59133172 | solution.py:39
  188.8 9.5 fusion.196
  265.0 16.6 %all-reduce.13.cloned.1.call-done = f32[1216,768]{1,0:T(8,128)} async-done(((f32[1216,768]{1,0:T(8,128)}), f32[1216,768]{1,0:T(8,128)}) %all-reduce.13.cloned.1.call-update) | async-done | bytes 3735568 | tf_op jit(solution)/shard_map/psum | solution.py:160
  288.1 10.5 convert_reduce_fusion
  305.6 25.6 %all-reduce.15.cloned.1.call-done = f32[1216,768]{1,0:T(8,128)} async-done(((f32[1216,768]{1,0:T(8,128)}), f32[1216,768]{1,0:T(8,128)}) %all-reduce.15.cloned.1.call-update) | async-done | bytes 3735568 | tf_op jit(solution)/shard_map/psum | solution.py:173
  352.9 127.3 %while.39 = (s32[]{:T(128)}, f32[1216,6,64]{0,2,1:T(8,128)}, f32[1216,6,64]{0,2,1:T(8,128)}, bf16[2,608,6,64]{1,3,2,0:T(8,128)(2,1)}, bf16[2,608,6,64]{1,3,2,0:T...) while((s32[]{:T(128)}, f32[1216,6,64]{0,2,1:T(8,128)}, ...), condition=%wide.region_24.25_spmd.clone, body=%wide.region_22.24_spmd.clone.sunk | while | flops 2882247168 | bytes 270494848 | solution.py:82
  353.6 10.4 fusion.208
  364.0 17.0 %multiply_reduce_fusion.10 = (f32[6,608]{1,0:T(8,128)S(1)}, f32[6,608,1216]{2,1,0:T(8,128)}) fusion(f32[6,608,1216]{2,1,0:T(8,128)} %fusion.208, f32[6,608]{1,0:T(8,128)S(1)} %dynamic-slice_bitcast_fusion.2, bf16[1216,6,64]{0,2,1:T(8,128)(2,1)S(1)} %get-tuple-element.642, bf16[2,608,6,64]{1,3,2,0:T(8,128)(2,1)S(1)} %get-tuple-element.639, ...), kind=kOutput, calls=%fused_computation.44.clone.1 | convolution fusion | flops 589980096 | bytes 37775620 | tf_op jit(solution)/shard_map/while/body/eval_jaxpr/qhe,khe->hqk/dot_general | solution.py:17
  381.0 16.5 %multiply_convert_fusion.4 = bf16[6,608,1216]{2,1,0:T(8,128)(2,1)} fusion(f32[6,608,1216]{2,1,0:T(8,128)} %get-tuple-element.556, f32[6,608,1216]{2,1,0:T(8,128)} %fusion.208, f32[6,608]{1,0:T(8,128)S(1)} %get-tuple-element.557), kind=kLoop, calls=%fused_computation.43.clone.1 | loop fusion | flops 13307904 | bytes 44374272 | tf_op jit(solution)/shard_map/while/body/eval_jaxpr/convert_element_type | solution.py:63
  416.8 10.4 fusion.208
  427.2 17.0 %multiply_reduce_fusion.10 = (f32[6,608]{1,0:T(8,128)S(1)}, f32[6,608,1216]{2,1,0:T(8,128)}) fusion(f32[6,608,1216]{2,1,0:T(8,128)} %fusion.208, f32[6,608]{1,0:T(8,128)S(1)} %dynamic-slice_bitcast_fusion.2, bf16[1216,6,64]{0,2,1:T(8,128)(2,1)S(1)} %get-tuple-element.642, bf16[2,608,6,64]{1,3,2,0:T(8,128)(2,1)S(1)} %get-tuple-element.639, ...), kind=kOutput, calls=%fused_computation.44.clone.1 | convolution fusion | flops 589980096 | bytes 37775620 | tf_op jit(solution)/shard_map/while/body/eval_jaxpr/qhe,khe->hqk/dot_general | solution.py:17
  444.2 16.5 %multiply_convert_fusion.4 = bf16[6,608,1216]{2,1,0:T(8,128)(2,1)} fusion(f32[6,608,1216]{2,1,0:T(8,128)} %get-tuple-element.556, f32[6,608,1216]{2,1,0:T(8,128)} %fusion.208, f32[6,608]{1,0:T(8,128)S(1)} %get-tuple-element.557), kind=kLoop, calls=%fused_computation.43.clone.1 | loop fusion | flops 13307904 | bytes 44374272 | tf_op jit(solution)/shard_map/while/body/eval_jaxpr/convert_element_type | solution.py:63
  496.8 25.0 %all-reduce.17.cloned.1.call-done = f32[1216,768]{1,0:T(8,128)} async-done(((f32[1216,768]{1,0:T(8,128)}), f32[1216,768]{1,0:T(8,128)}) %all-reduce.17.cloned.1.call-update) | async-done | bytes 3735568 | tf_op jit(solution)/shard_map/psum | solution.py:193
  568.4 77.0 %all-reduce.2 = (f32[2,384]{1,0:T(2,128)S(1)}, f32[1536]{0:T(1024)S(1)}) all-reduce(f32[2,384]{1,0:T(2,128)S(1)} %pad_maximum_fusion.1, f32[1536]{0:T(1024)S(1)} %copy-done.63), channel_id=4, replica_groups=mesh['batch'=16,'tp'=2] {'batch'}, use_global_device_ids=true, to_apply=%region_38.39.clone | all-reduce | flops 2304 | bytes 18432
  659.3 123.5 %reduce-scatter.11.cloned.1.call-done = f32[384,48]{0,1:T(8,128)} async-done(((f32[384,768]{0,1:T(8,128)}), f32[384,48]{0,1:T(8,128)}) %reduce-scatter.11.cloned.1.call-update) | async-done | bytes 73744 | tf_op jit(solution)/shard_map/reduce_scatter | solution.py:203
  782.9 141.6 %reduce-scatter.13.cloned.1.call-done = f32[48,1536]{1,0:T(8,128)} async-done(((f32[768,1536]{1,0:T(8,128)}), f32[48,1536]{1,0:T(8,128)}) %reduce-scatter.13.cloned.1.call-update) | async-done | bytes 294928 | tf_op jit(solution)/shard_map/reduce_scatter | solution.py:204
  924.5 142.8 %reduce-scatter.15.cloned.1.call-done = f32[1536,48]{0,1:T(8,128)} async-done(((f32[1536,768]{0,1:T(8,128)}), f32[1536,48]{0,1:T(8,128)}) %reduce-scatter.15.cloned.1.call-update) | async-done | bytes 294928 | tf_op jit(solution)/shard_map/reduce_scatter | solution.py:206
  1067.2 138.2 %reduce-scatter.9.cloned.1.call-done = f32[48,3,384]{2,0,1:T(8,128)} async-done(((f32[768,3,384]{2,0,1:T(8,128)}), f32[48,3,384]{2,0,1:T(8,128)}) %reduce-scatter.9.cloned.1.call-update) | async-done | bytes 221200 | tf_op jit(solution)/shard_map/reduce_scatter | solution.py:201
  (321 shorter events, 315.6 us)
Async XLA Ops:
  7.2 108.7 %copy-start = (bf16[768,1536]{1,0:T(8,128)(2,1)S(1)}, bf16[768,1536]{1,0:T(8,128)(2,1)}, u32[]{:S(2)}) copy-start(bf16[768,1536]{1,0:T(8,128)(2,1)} %param.32) | copy-start | bytes 7077892
  7.2 103.4 %all-reduce.9.cloned.1.call-start = ((), (), s32[]{:S(2)}) async-start(), calls=%async_computation.5 | async-start | bytes 7471104 | tf_op jit(solution)/shard_map/psum | solution.py:131
  83.4 27.2 %copy-start.46 = (f32[768]{0:T(1024)S(1)}, f32[768]{0:T(1024)}, u32[]{:S(2)}) copy-start(f32[768]{0:T(1024)} %param.29) | copy-start | bytes 9220
  83.4 69.0 %all-reduce.11.cloned.1.call-start = ((), (), s32[]{:S(2)}) async-start(), calls=%async_computation.6 | async-start | bytes 7471104 | tf_op jit(solution)/shard_map/psum | solution.py:137
  126.7 25.7 %copy-start.64 = (f32[768]{0:T(1024)S(1)}, f32[768]{0:T(1024)}, u32[]{:S(2)}) copy-start(f32[768]{0:T(1024)} %param.35) | copy-start | bytes 9220
  126.7 154.9 %all-reduce.13.cloned.1.call-start = ((), (), s32[]{:S(2)}) async-start(), calls=%async_computation.7 | async-start | bytes 7471104 | tf_op jit(solution)/shard_map/psum | solution.py:160
  255.9 25.7 %copy-start.47 = (f32[768]{0:T(1024)S(1)}, f32[768]{0:T(1024)}, u32[]{:S(2)}) copy-start(f32[768]{0:T(1024)} %param.29) | copy-start | bytes 9220
  255.9 75.3 %all-reduce.15.cloned.1.call-start = ((), (), s32[]{:S(2)}) async-start(), calls=%async_computation.8 | async-start | bytes 7471104 | tf_op jit(solution)/shard_map/psum | solution.py:173
  285.4 51.0 %copy-start.36 = (f32[1216]{0:T(1024)}, f32[1216]{0:T(1024)S(1)}, u32[]{:S(2)}) copy-start(f32[1216]{0:T(1024)S(1)} %broadcast_multiply_fusion) | copy-start | bytes 14596
  288.1 48.4 %copy-start.40 = (f32[1216]{0:T(1024)}, f32[1216]{0:T(1024)S(1)}, u32[]{:S(2)}) copy-start(f32[1216]{0:T(1024)S(1)} %fusion.101) | copy-start | bytes 14596
  305.6 216.3 %all-reduce.17.cloned.1.call-start = ((), (), s32[]{:S(2)}) async-start(), calls=%async_computation.9 | async-start | bytes 7471104 | tf_op jit(solution)/shard_map/psum | solution.py:193
  381.0 20.4 %copy-start.2 = (f32[6,608,1216]{2,1,0:T(8,128)S(1)}, f32[6,608,1216]{2,1,0:T(8,128)}, u32[]{:S(2)}) copy-start(f32[6,608,1216]{2,1,0:T(8,128)} %get-tuple-element.556) | copy-start | bytes 53231620 | tf_op jit(solution)/shard_map/while
  444.2 20.4 %copy-start.2 = (f32[6,608,1216]{2,1,0:T(8,128)S(1)}, f32[6,608,1216]{2,1,0:T(8,128)}, u32[]{:S(2)}) copy-start(f32[6,608,1216]{2,1,0:T(8,128)} %get-tuple-element.556) | copy-start | bytes 53231620 | tf_op jit(solution)/shard_map/while
  496.1 25.7 %copy-start.6 = (bf16[1216,768]{1,0:T(8,128)(2,1)S(1)}, bf16[1216,768]{1,0:T(8,128)(2,1)}, u32[]{:S(2)}) copy-start(bf16[1216,768]{1,0:T(8,128)(2,1)} %param.21) | copy-start | bytes 5603332
  496.1 25.7 %copy-start.33 = (f32[1216]{0:T(1024)S(1)}, f32[1216]{0:T(1024)}, u32[]{:S(2)}) copy-start(f32[1216]{0:T(1024)} %copy-done.32) | copy-start | bytes 14596
  496.2 25.7 %copy-start.50 = (f32[768]{0:T(1024)S(1)}, f32[768]{0:T(1024)}, u32[]{:S(2)}) copy-start(f32[768]{0:T(1024)} %param.24) | copy-start | bytes 9220
  496.2 29.0 %copy-start.43 = (f32[1216]{0:T(1024)S(1)}, f32[1216]{0:T(1024)}, u32[]{:S(2)}) copy-start(f32[1216]{0:T(1024)} %copy-done.42) | copy-start | bytes 14596
  496.2 29.0 %copy-start.39 = (f32[1216]{0:T(1024)S(1)}, f32[1216]{0:T(1024)}, u32[]{:S(2)}) copy-start(f32[1216]{0:T(1024)} %copy-done.38) | copy-start | bytes 14596
  496.2 158.5 %reduce-scatter.17.cloned.1.call-start = ((), (), s32[]{:S(2)}) async-start(), calls=%async_computation.14 | async-start | bytes 417792
  531.8 251.1 %reduce-scatter.11.cloned.1.call-start = ((), (), s32[]{:S(2)}) async-start(), calls=%async_computation.11 | async-start | bytes 1253376 | tf_op jit(solution)/shard_map/reduce_scatter | solution.py:203
  535.6 388.9 %reduce-scatter.13.cloned.1.call-start = ((), (), s32[]{:S(2)}) async-start(), calls=%async_computation.12 | async-start | bytes 5013504 | tf_op jit(solution)/shard_map/reduce_scatter | solution.py:204
  544.7 522.6 %reduce-scatter.15.cloned.1.call-start = ((), (), s32[]{:S(2)}) async-start(), calls=%async_computation.13 | async-start | bytes 5013504 | tf_op jit(solution)/shard_map/reduce_scatter | solution.py:206
  555.1 650.4 %reduce-scatter.9.cloned.1.call-start = ((), (), s32[]{:S(2)}) async-start(), calls=%async_computation.10 | async-start | bytes 3760128 | tf_op jit(solution)/shard_map/reduce_scatter | solution.py:201
  565.6 639.8 %copy-start.1 = (bf16[768,1536]{1,0:T(8,128)(2,1)S(1)}, bf16[768,1536]{1,0:T(8,128)(2,1)}, u32[]{:S(2)}) copy-start(bf16[768,1536]{1,0:T(8,128)(2,1)} %param.32) | copy-start | bytes 7077892
  (67 other events, 245.2 us)
Sparse Core Ops, SparseCore 0:
  83.5 27.0 all-reduce.8
  126.8 25.5 all-reduce.10
  256.0 25.5 all-reduce.12
  305.7 25.5 all-reduce.14
  496.3 25.5 all-reduce.16
  531.9 122.7 reduce-scatter.16
  660.0 122.7 reduce-scatter.10
  788.6 135.8 reduce-scatter.12
  931.1 136.1 reduce-scatter.14
  1072.8 132.6 reduce-scatter.8
where the time goes:
time: 1220 us; the launch traced here: 1210 us
  waiting for transfers between devices  671 us (55%)
  matrix products  245 us (20%)
  other arithmetic  109 us (9%)
  local copies, waits for them, and re-layouts  92.3 us (8%)
  blocking collectives  77 us (6%)
  between operations  16.9 us (1%)
    reduce_scatter x1, waiting for transfers between devices, shards(): lax.psum_scatter(w_back_grad, 'batch', scatter_dimension=1, tiled=True)  143 us
    reduce_scatter x1, waiting for transfers between devices, shards(): lax.psum_scatter(w_in_grad, 'batch', scatter_dimension=0, tiled=True)  142 us
    reduce_scatter x1, waiting for transfers between devices, shards(): lax.psum_scatter(w_qkv_grad, 'batch', scatter_dimension=0, tiled=True)  138 us
    reduce_scatter x1, waiting for transfers between devices, shards(): lax.psum_scatter(w_out_grad, 'batch', scatter_dimension=1, tiled=True)  124 us
    unnamed x1, blocking collectives  77 us
    dot_general x4, matrix products, masked_scores(): jnp.einsum('qhe,khe->hqk', rows, keys, preferred_element_type=jnp.float32)  53 us
    psum x2, waiting for transfers between devices, shards(): summed = lax.psum(partial_out, 'tp')  43.7 us
    dot_general x4, matrix products, one_block(): jnp.einsum('hqk,khe->qhe', weights, values, preferred_element_type=jnp.fl...  39.4 us
  transfers between devices with their start and end apart: 10, of which 10 were waited for; matrix products, arithmetic and copies ran while one was open for 4% of the time, Pallas kernels for 0%

commit v1 on v0

v1 whole, which is shorter than its diff:
```python
import functools

import jax
import jax.numpy as jnp
from jax import lax
from jax.experimental import pallas as pl
from jax.experimental.pallas import tpu as pltpu
from jax.sharding import PartitionSpec as P

HEAD_DIM = 64
PAIR = 2 * HEAD_DIM
HALF = 608
TILE = 304
WINDOWS = ((0, 688), (448, 1216))
f32 = jnp.float32
bf16 = jnp.bfloat16


def params(mib):
    return pltpu.CompilerParams(vmem_limit_bytes=mib << 20)


def cost(flops, nbytes, trans=0):
    return pl.CostEstimate(flops=int(flops), bytes_accessed=int(nbytes), transcendentals=int(trans))


def nn(a, b):
    return jnp.dot(a, b, preferred_element_type=f32)


def nt(a, b):
    return lax.dot_general(a, b, (((1,), (1,)), ((), ())), preferred_element_type=f32)


def tn(a, b):
    return lax.dot_general(a, b, (((0,), (0,)), ((), ())), preferred_element_type=f32)


def standardize(values):
    center = values - jnp.mean(values, -1, keepdims=True)
    spread = jnp.mean(center * center, -1, keepdims=True)
    inv = lax.rsqrt(spread + 1e-06)
    return center * inv, inv


def norm_back(unit, inv, gain, grad):
    scaled = grad * gain
    return inv * (
        scaled
        - jnp.mean(scaled, -1, keepdims=True)
        - unit * jnp.mean(scaled * unit, -1, keepdims=True)
    )


def whole(shape):
    return pl.BlockSpec(shape, lambda *_: (0,) * len(shape))


def project_kernel(x_ref, gain_ref, shift_ref, w_ref, bias_ref, n_ref, q_ref, k_ref, v_ref):
    unit, _ = standardize(x_ref[...].astype(f32))
    normed = (unit * gain_ref[...] + shift_ref[...]).astype(bf16)
    n_ref[...] = normed
    scale = HEAD_DIM ** (-0.5)
    q_ref[...] = ((nn(normed, w_ref[0]) + bias_ref[0:1]).astype(bf16).astype(f32) * scale).astype(bf16)
    k_ref[...] = nn(normed, w_ref[1]).astype(bf16)
    v_ref[...] = (nn(normed, w_ref[2]) + bias_ref[1:2]).astype(bf16)


def project(tokens, gain, shift, w3, qv_bias):
    tok, dim = tokens.shape
    width = w3.shape[2]
    rows = lambda n: pl.BlockSpec((TILE, n), lambda i: (i, 0))
    out = jax.ShapeDtypeStruct((tok, width), bf16)
    return pl.pallas_call(
        project_kernel,
        grid=(tok // TILE,),
        in_specs=[rows(dim), whole((1, dim)), whole((1, dim)), whole(w3.shape), whole((2, width))],
        out_specs=[rows(dim), rows(width), rows(width), rows(width)],
        out_shape=[jax.ShapeDtypeStruct((tok, dim), bf16), out, out, out],
        compiler_params=params(32),
        cost_estimate=cost(2 * tok * dim * 3 * width, tok * (2 * dim + 3 * width) * 2 + w3.size * 2),
        name="project",
    )(tokens, gain, shift, w3, qv_bias)


def attend_kernel(half, q_ref, k_ref, v_ref, col_ref, row_ref, w_ref, *refs):
    o_ref, lse_ref, part_ref, mask_ref = refs[-4:]
    low, high = WINDOWS[half]
    step = pl.program_id(0)

    @pl.when(step == 0)
    def _():
        same = col_ref[...] == row_ref[:, low:high]
        mask_ref[...] = jnp.where(same, 0.0, -1000000000.0)

    first = lax.broadcasted_iota(jnp.int32, (1, PAIR), 1) < HEAD_DIM
    keys = k_ref[low:high, :]
    values = v_ref[low:high, :]
    zero = jnp.zeros((), bf16)
    one = jnp.ones((), bf16)
    with_ones = (jnp.where(first, values, one), jnp.where(first, one, values))
    for at in range(0, HALF, TILE):
        rows = q_ref[at : at + TILE, :]
        mask = mask_ref[at : at + TILE, :]
        outs, logs = [], []
        for head in range(2):
            own = jnp.where(first, rows, zero) if head == 0 else jnp.where(first, zero, rows)
            scores = nt(own, keys) + mask
            top = jnp.max(scores, -1, keepdims=True)
            expo = jnp.exp(scores - top).astype(bf16)
            mixed = nn(expo, with_ones[head])
            total = pltpu.roll(mixed, HEAD_DIM, 1)
            outs.append(mixed / total)
            logs.append(top + jnp.log(total))
        mixed = jnp.where(first, outs[0], outs[1]).astype(bf16)
        o_ref[at : at + TILE, :] = mixed
        lse_ref[at : at + TILE, :] = jnp.where(first, logs[0], logs[1])
        part = nn(mixed, w_ref[...])

        @pl.when(step == 0)
        def _():
            part_ref[at : at + TILE, :] = part

        @pl.when(step > 0)
        def _():
            part_ref[at : at + TILE, :] += part


def attend(half, q, k, v, ids_col, ids_row, w_out, before=()):
    tok, width = q.shape
    dim = w_out.shape[1]
    low, high = WINDOWS[half]
    pair_rows = pl.BlockSpec((HALF, PAIR), lambda p: (half, p))
    pair_all = pl.BlockSpec((tok, PAIR), lambda p: (0, p))
    return pl.pallas_call(
        functools.partial(attend_kernel, half),
        grid=(width // PAIR,),
        in_specs=[
            pair_rows,
            pair_all,
            pair_all,
            pl.BlockSpec((HALF, 1), lambda p: (half, 0)),
            whole((1, tok)),
            pl.BlockSpec((PAIR, dim), lambda p: (p, 0)),
        ]
        + [pl.BlockSpec(memory_space=pl.ANY)] * len(before),
        out_specs=[pair_rows, pair_rows, whole((HALF, dim))],
        out_shape=[
            jax.ShapeDtypeStruct((tok, width), bf16),
            jax.ShapeDtypeStruct((tok, width), f32),
            jax.ShapeDtypeStruct((HALF, dim), f32),
        ],
        scratch_shapes=[pltpu.VMEM((HALF, high - low), f32)],
        input_output_aliases={6 + i: i for i in range(len(before))},
        compiler_params=params(48),
        cost_estimate=cost(16 * HALF * (high - low) * width, tok * width * 6 + HALF * dim * 4),
        name="attend",
    )(q, k, v, ids_col, ids_row, w_out, *before)


def hidden_kernel(x_ref, own_ref, peer_ref, ob_ref, gain_ref, shift_ref, w_ref, ib_ref, *refs):
    mid_ref, n_ref, hid_ref, slope_ref = refs[-4:]
    middle = x_ref[...].astype(f32) + (own_ref[...] + peer_ref[...]) + ob_ref[...]
    mid_ref[...] = middle
    unit, _ = standardize(middle)
    normed = (unit * gain_ref[...] + shift_ref[...]).astype(bf16)
    n_ref[...] = normed
    width = w_ref.shape[1]
    piece = 512
    c0 = 0.7978845608028654
    for at in range(0, width, piece):
        u = nn(normed, w_ref[:, at : at + piece]) + ib_ref[:, at : at + piece]
        sq = u * u
        t = jnp.tanh(u * (c0 + (c0 * 0.044715) * sq))
        cdf = 0.5 + 0.5 * t
        hid_ref[:, at : at + piece] = (u * cdf).astype(bf16)
        slope = cdf + (0.5 * u) * (1.0 - t * t) * (c0 + (3.0 * 0.044715 * c0) * sq)
        slope_ref[:, at : at + piece] = slope.astype(bf16)


def hidden_layer(half, tokens, own, peer, out_bias, gain, shift, w_in, in_bias, before=()):
    tok, dim = tokens.shape
    width = w_in.shape[1]
    per = HALF // TILE
    glob = lambda n: pl.BlockSpec((TILE, n), lambda i: (i + per * half, 0))
    loc = lambda n: pl.BlockSpec((TILE, n), lambda i: (i, 0))
    return pl.pallas_call(
        hidden_kernel,
        grid=(per,),
        in_specs=[
            glob(dim),
            loc(dim),
            loc(dim),
            whole((1, dim)),
            whole((1, dim)),
            whole((1, dim)),
            whole(w_in.shape),
            whole((1, width)),
        ]
        + [pl.BlockSpec(memory_space=pl.ANY)] * len(before),
        out_specs=[glob(dim), glob(dim), glob(width), glob(width)],
        out_shape=[
            jax.ShapeDtypeStruct((tok, dim), f32),
            jax.ShapeDtypeStruct((tok, dim), bf16),
            jax.ShapeDtypeStruct((tok, width), bf16),
            jax.ShapeDtypeStruct((tok, width), bf16),
        ],
        input_output_aliases={8 + i: i for i in range(len(before))},
        compiler_params=params(40),
        cost_estimate=cost(2 * HALF * dim * width, HALF * (dim * 16 + width * 4) + w_in.size * 2, HALF * width),
        name="hidden_layer",
    )(tokens, own, peer, out_bias, gain, shift, w_in, in_bias, *before)


def matmul_kernel(a_ref, b_ref, o_ref):
    o_ref[...] = nn(a_ref[...], b_ref[...])


def rows_matmul(a, b):
    tok, depth = a.shape
    width = b.shape[1]
    return pl.pallas_call(
        matmul_kernel,
        grid=(tok // TILE,),
        in_specs=[pl.BlockSpec((TILE, depth), lambda i: (i, 0)), whole(b.shape)],
        out_specs=pl.BlockSpec((TILE, width), lambda i: (i, 0)),
        out_shape=jax.ShapeDtypeStruct((tok, width), f32),
        compiler_params=params(32),
        cost_estimate=cost(2 * tok * depth * width, tok * (depth * 2 + width * 4) + b.size * 2),
        name="mlp_out",
    )(a, b)


def hidden_back_kernel(g_ref, slope_ref, wb_ref, wi_ref, du_ref, dn_ref, db_ref, gb_ref):
    step = pl.program_id(0)
    grad = g_ref[...]
    width = slope_ref.shape[1]
    piece = 512
    total = None
    sums = []
    for at in range(0, width, piece):
        back = nt(grad, wb_ref[at : at + piece, :])
        du = (back * slope_ref[:, at : at + piece].astype(f32)).astype(bf16)
        du_ref[:, at : at + piece] = du
        sums.append(jnp.sum(du.astype(f32), 0, keepdims=True))
    dn_ref[...] = nt(du_ref[...], wi_ref[...])

    @pl.when(step == 0)
    def _():
        db_ref[...] = jnp.zeros_like(db_ref)
        gb_ref[...] = jnp.zeros_like(gb_ref)

    for i, at in enumerate(range(0, width, piece)):
        db_ref[:, at : at + piece] += sums[i]
    gb_ref[...] += jnp.sum(grad.astype(f32), 0, keepdims=True)


def hidden_back(cotangent, slope, w_back, w_in):
    tok, dim = cotangent.shape
    width = slope.shape[1]
    rows = lambda n: pl.BlockSpec((TILE, n), lambda i: (i, 0))
    return pl.pallas_call(
        hidden_back_kernel,
        grid=(tok // TILE,),
        in_specs=[rows(dim), rows(width), whole(w_back.shape), whole(w_in.shape)],
        out_specs=[rows(width), rows(dim), whole((1, width)), whole((1, dim))],
        out_shape=[
            jax.ShapeDtypeStruct((tok, width), bf16),
            jax.ShapeDtypeStruct((tok, dim), f32),
            jax.ShapeDtypeStruct((1, width), f32),
            jax.ShapeDtypeStruct((1, dim), f32),
        ],
        compiler_params=params(40),
        cost_estimate=cost(4 * tok * dim * width, tok * (dim * 6 + width * 4) + w_in.size * 4),
        name="hidden_back",
    )(cotangent, slope, w_back, w_in)


def middle_back_kernel(mid_ref, own_ref, peer_ref, g_ref, gain_ref, w_ref, dh_ref, dr_ref, do_ref, sum_ref):
    step = pl.program_id(0)
    unit, inv = standardize(mid_ref[...])
    grad = own_ref[...] + peer_ref[...]
    dh = g_ref[...].astype(f32) + norm_back(unit, inv, gain_ref[...], grad)
    dh_ref[...] = dh
    dr = dh.astype(bf16)
    dr_ref[...] = dr
    do_ref[...] = nt(dr, w_ref[...]).astype(bf16)

    @pl.when(step == 0)
    def _():
        sum_ref[...] = jnp.zeros_like(sum_ref)

    sum_ref[0:1] += jnp.sum(grad * unit, 0, keepdims=True)
    sum_ref[1:2] += jnp.sum(grad, 0, keepdims=True)
    sum_ref[2:3] += jnp.sum(dr.astype(f32), 0, keepdims=True)


def middle_back(middle, own, peer, cotangent, gain, w_out):
    tok, dim = middle.shape
    width = w_out.shape[0]
    rows = lambda n: pl.BlockSpec((TILE, n), lambda i: (i, 0))
    return pl.pallas_call(
        middle_back_kernel,
        grid=(tok // TILE,),
        in_specs=[rows(dim), rows(dim), rows(dim), rows(dim), whole((1, dim)), whole(w_out.shape)],
        out_specs=[rows(dim), rows(dim), rows(width), whole((8, dim))],
        out_shape=[
            jax.ShapeDtypeStruct((tok, dim), f32),
            jax.ShapeDtypeStruct((tok, dim), bf16),
            jax.ShapeDtypeStruct((tok, width), bf16),
            jax.ShapeDtypeStruct((8, dim), f32),
        ],
        compiler_params=params(32),
        cost_estimate=cost(2 * tok * dim * width, tok * (dim * 20 + width * 2) + w_out.size * 2),
        name="middle_back",
    )(middle, own, peer, cotangent, gain, w_out)


def attend_back_kernel(q_ref, k_ref, v_ref, do_ref, lse_ref, col_ref, row_ref, dq_ref, dk_ref, dv_ref, sum_ref, acc_k, acc_v):
    first = lax.broadcasted_iota(jnp.int32, (1, PAIR), 1) < HEAD_DIM
    zero = jnp.zeros((), bf16)
    for half in range(2):
        low, high = WINDOWS[half]
        span = slice(half * HALF, half * HALF + HALF)
        rows = q_ref[span, :]
        grads = do_ref[span, :]
        keys = k_ref[low:high, :]
        values = v_ref[low:high, :]
        logs = jnp.transpose(lse_ref[span, :])
        mask = jnp.where(col_ref[low:high, :] == row_ref[:, span], 0.0, -1000000000.0)
        parts = []
        for head in range(2):
            pick = lambda a: jnp.where(first, a, zero) if head == 0 else jnp.where(first, zero, a)
            lse = logs[head * HEAD_DIM : head * HEAD_DIM + 1, :]
            probs = jnp.exp(nt(keys, pick(rows)) + mask - lse)
            back = nt(values, pick(grads))
            inner = jnp.sum(probs * back, 0, keepdims=True)
            slant = (probs * (back - inner)).astype(bf16)
            dv = nn(probs.astype(bf16), grads)
            dk = nn(slant, rows)
            dq = tn(slant, keys)
            parts.append((dq, dk, dv))
        dq, dk, dv = (jnp.where(first, a, b) for a, b in zip(*parts))
        dq = (dq * HEAD_DIM ** (-0.5)).astype(bf16)
        dq_ref[span, :] = dq
        top = jnp.sum(dq.astype(f32), 0, keepdims=True)
        if half == 0:
            sum_ref[...] = jnp.zeros_like(sum_ref)
            acc_k[low:high, :] = dk
            acc_v[low:high, :] = dv
        else:
            edge = WINDOWS[0][1]
            acc_k[low:edge, :] += dk[: edge - low]
            acc_v[low:edge, :] += dv[: edge - low]
            acc_k[edge:high, :] = dk[edge - low :]
            acc_v[edge:high, :] = dv[edge - low :]
        sum_ref[0:1, :] += top
    dk_ref[...] = acc_k[...].astype(bf16)
    dv = acc_v[...].astype(bf16)
    dv_ref[...] = dv
    sum_ref[1:2, :] = jnp.sum(dv.astype(f32), 0, keepdims=True)


def attend_back(q, k, v, do, lse, ids_col, ids_row):
    tok, width = q.shape
    pair = pl.BlockSpec((tok, PAIR), lambda p: (0, p))
    out = jax.ShapeDtypeStruct((tok, width), bf16)
    return pl.pallas_call(
        attend_back_kernel,
        grid=(width // PAIR,),
        in_specs=[pair, pair, pair, pair, pair, whole((tok, 1)), whole((1, tok))],
        out_specs=[pair, pair, pair, pl.BlockSpec((8, PAIR), lambda p: (0, p))],
        out_shape=[out, out, out, jax.ShapeDtypeStruct((8, width), f32)],
        scratch_shapes=[pltpu.VMEM((tok, PAIR), f32), pltpu.VMEM((tok, PAIR), f32)],
        compiler_params=params(56),
        cost_estimate=cost(4 * 10 * tok * HALF * width, tok * width * 18),
        name="attend_back",
    )(q, k, v, do, lse, ids_col, ids_row)


def normed_back_kernel(dq_ref, dk_ref, dv_ref, w_ref, o_ref):
    o_ref[...] = nt(dq_ref[...], w_ref[0]) + nt(dk_ref[...], w_ref[1]) + nt(dv_ref[...], w_ref[2])


def normed_back(dq, dk, dv, w3):
    tok, width = dq.shape
    dim = w3.shape[1]
    rows = lambda n: pl.BlockSpec((TILE, n), lambda i: (i, 0))
    return pl.pallas_call(
        normed_back_kernel,
        grid=(tok // TILE,),
        in_specs=[rows(width), rows(width), rows(width), whole(w3.shape)],
        out_specs=rows(dim),
        out_shape=jax.ShapeDtypeStruct((tok, dim), f32),
        compiler_params=params(32),
        cost_estimate=cost(6 * tok * dim * width, tok * (dim * 4 + width * 6) + w3.size * 2),
        name="normed_back",
    )(dq, dk, dv, w3)


def input_back_kernel(x_ref, own_ref, peer_ref, dh_ref, gain_ref, o_ref, sum_ref):
    step = pl.program_id(0)
    unit, inv = standardize(x_ref[...].astype(f32))
    grad = own_ref[...] + peer_ref[...]
    o_ref[...] = (dh_ref[...] + norm_back(unit, inv, gain_ref[...], grad)).astype(bf16)

    @pl.when(step == 0)
    def _():
        sum_ref[...] = jnp.zeros_like(sum_ref)

    sum_ref[0:1] += jnp.sum(grad * unit, 0, keepdims=True)
    sum_ref[1:2] += jnp.sum(grad, 0, keepdims=True)


def input_back(tokens, own, peer, dh, gain):
    tok, dim = tokens.shape
    rows = pl.BlockSpec((TILE, dim), lambda i: (i, 0))
    return pl.pallas_call(
        input_back_kernel,
        grid=(tok // TILE,),
        in_specs=[rows, rows, rows, rows, whole((1, dim))],
        out_specs=[rows, whole((8, dim))],
        out_shape=[jax.ShapeDtypeStruct((tok, dim), bf16), jax.ShapeDtypeStruct((8, dim), f32)],
        compiler_params=params(32),
        cost_estimate=cost(20 * tok * dim, tok * dim * 16),
        name="input_back",
    )(tokens, own, peer, dh, gain)


def grad_kernel(parts, group, place_ref, a_ref, b_ref, *refs):
    outs, turned = refs[:parts], refs[parts]

    @pl.when(pl.program_id(0) == 0)
    def _():
        flat = jnp.transpose(a_ref[...])
        if group:
            for g in range(flat.shape[0] // group):
                at = pl.multiple_of(place_ref[g] * group, group)
                turned[pl.ds(at, group), :] = flat[g * group : (g + 1) * group, :]
        else:
            turned[...] = flat

    total = nn(turned[...], b_ref[...])
    rows = total.shape[0] // parts
    for i, out in enumerate(outs):
        out[...] = total[i * rows : (i + 1) * rows, :]


def weight_grad(parts, place, a, b):
    tok, dim = a.shape
    width = b.shape[1]
    step = 384
    count = place.shape[0]
    group = dim // count
    if group % 16:
        order = jnp.argsort(place)
        rows = (order[:, None] * group + jnp.arange(group)[None, :]).reshape(dim)
        a = jnp.take(a, rows, axis=1)
        group = 0
    rows = dim // parts
    return pl.pallas_call(
        functools.partial(grad_kernel, parts, group),
        grid_spec=pltpu.PrefetchScalarGridSpec(
            num_scalar_prefetch=1,
            grid=(width // step,),
            in_specs=[
                pl.BlockSpec((tok, dim), lambda i, *_: (0, 0)),
                pl.BlockSpec((tok, step), lambda i, *_: (0, i)),
            ],
            out_specs=[pl.BlockSpec((rows, step), lambda i, *_: (0, i))] * parts,
            scratch_shapes=[pltpu.VMEM((dim, tok), bf16)],
        ),
        out_shape=[jax.ShapeDtypeStruct((rows, width), f32)] * parts,
        compiler_params=params(40),
        cost_estimate=cost(2 * tok * dim * width, tok * (dim + width) * 2 + dim * width * 4),
        name="weight_grad",
    )(place, a, b)


class Exchange:
    def __init__(self, batch):
        side = 1
        while side * side * 4 < batch:
            side *= 2
        self.batch = batch
        sizes = (batch // (side * side), side, side)
        strides = (side * side, side, 1)
        axes = list(zip(sizes, strides))
        slow, mid, fast = axes
        self.orders = ((fast, mid, slow), (mid, fast, slow))
        me = lax.axis_index("batch")
        core = lax.axis_index("tp")
        away = jnp.arange(batch, dtype=jnp.int32) ^ me
        places = []
        for order in self.orders:
            place = jnp.zeros_like(away)
            for size, stride in order:
                place = place * size + (away // stride) % size
            places.append(place)
        self.place = jnp.where(core == 0, places[0], places[1]).astype(jnp.int32)

    def first_parts(self):
        return self.orders[0][0][0]

    def swap(self, block, phase, k):
        perm = []
        for i in range(self.batch):
            for core in range(2):
                _, stride = self.orders[core][phase]
                perm.append((2 * i + core, 2 * (i ^ (k * stride)) + core))
        return lax.ppermute(block, ("batch", "tp"), perm)

    def reduce(self, parts):
        for phase in range(3):
            got = [self.swap(parts[k], phase, k) for k in range(1, len(parts))]
            if phase == 2:
                total = parts[0]
                for g in got:
                    total = total + g
                return total
            size = self.orders[0][phase + 1][0]
            rows = parts[0].shape[0] // size
            cut = lambda a, i: lax.slice_in_dim(a, i * rows, (i + 1) * rows, axis=0)
            following = []
            for i in range(size):
                total = cut(parts[0], i)
                for g in got:
                    total = total + cut(g, i)
                following.append(total)
            parts = following


def other_core(values):
    return lax.ppermute(values, "tp", [(0, 1), (1, 0)])


def shards(
    tokens,
    seq_ids,
    cotangent,
    norm1_gain,
    norm1_shift,
    w_qkv,
    qv_bias,
    w_out,
    out_bias,
    norm2_gain,
    norm2_shift,
    w_in,
    in_bias,
    w_back,
    back_bias,
    batch,
):
    tok, dim = tokens.shape
    row = lambda a: a.reshape(1, -1)
    ids_col, ids_row = seq_ids.reshape(tok, 1), seq_ids.reshape(1, tok)
    w3 = jnp.transpose(w_qkv, (1, 0, 2))
    exchange = Exchange(batch)
    parts = exchange.first_parts()

    normed, q, k, v = project(tokens, row(norm1_gain), row(norm1_shift), w3, qv_bias)
    mixed, lse, part_a = attend(0, q, k, v, ids_col, ids_row, w_out)
    peer_a = other_core(part_a)
    mixed, lse, part_b = attend(1, q, k, v, ids_col, ids_row, w_out, (mixed, lse))
    peer_b = other_core(part_b)
    mlp = (row(out_bias), row(norm2_gain), row(norm2_shift), w_in, row(in_bias))
    state = hidden_layer(0, tokens, part_a, peer_a, *mlp)
    state = hidden_layer(1, tokens, part_b, peer_b, *mlp, before=tuple(state))
    middle, normed_two, hidden, slope = state

    back_parts = weight_grad(parts, exchange.place, cotangent, hidden)
    du, dn2, in_bias_sum, back_bias_sum = hidden_back(cotangent, slope, w_back, w_in)
    dn2_peer = other_core(dn2)
    in_parts = weight_grad(parts, exchange.place, normed_two, du)
    mlp_own = rows_matmul(hidden, w_back)
    mlp_peer = other_core(mlp_own)
    dh, dr, do, middle_sums = middle_back(middle, dn2, dn2_peer, cotangent, row(norm2_gain), w_out)
    out_parts = weight_grad(parts, exchange.place, dr, mixed)
    layer_out = (middle + (mlp_own + mlp_peer) + back_bias).astype(bf16)
    dq, dk, dv, qv_sums = attend_back(q, k, v, do, lse, ids_col, ids_row)
    q_parts = weight_grad(parts, exchange.place, normed, dq)
    k_parts = weight_grad(parts, exchange.place, normed, dk)
    v_parts = weight_grad(parts, exchange.place, normed, dv)
    dn1 = normed_back(dq, dk, dv, w3)
    dn1_peer = other_core(dn1)
    tokens_grad, input_sums = input_back(tokens, dn1, dn1_peer, dh, row(norm1_gain))

    w_back_grad = jnp.transpose(exchange.reduce(back_parts))
    w_in_grad = exchange.reduce(in_parts)
    w_out_grad = jnp.transpose(exchange.reduce(out_parts))
    w_qkv_grad = jnp.stack([exchange.reduce(p) for p in (q_parts, k_parts, v_parts)], 1)

    pieces = [input_sums[0], input_sums[1], middle_sums[2], middle_sums[0], middle_sums[1], back_bias_sum[0]]
    pieces += [qv_sums[0], qv_sums[1], in_bias_sum[0]]
    packed = jnp.concatenate([p.reshape(batch, -1) for p in pieces], 1)
    vectors = lax.psum_scatter(packed, "batch", scatter_dimension=0, tiled=True)[0]
    out, at = [], 0
    for p in pieces:
        n = p.shape[0] // batch
        out.append(vectors[at : at + n])
        at += n
    n1g, n1s, obg, n2g, n2s, bbg, qb, vb, ibg = out
    return (
        layer_out,
        tokens_grad,
        n1g,
        n1s,
        w_qkv_grad,
        jnp.stack([qb, vb]),
        w_out_grad,
        obg,
        n2g,
        n2s,
        w_in_grad,
        ibg,
        w_back_grad,
        bbg,
    )


def solution(mesh):
    in_specs = (
        P("batch", None),
        P("batch"),
        P("batch", None),
        P(),
        P(),
        P(None, None, "tp"),
        P(None, "tp"),
        P("tp", None),
        P(),
        P(),
        P(),
        P(None, "tp"),
        P("tp"),
        P("tp", None),
        P(),
    )
    out_specs = (
        P("batch", None),
        P("batch", None),
        P("batch"),
        P("batch"),
        P("batch", None, "tp"),
        P(None, ("tp", "batch")),
        P("tp", "batch"),
        P("batch"),
        P("batch"),
        P("batch"),
        P("batch", "tp"),
        P(("tp", "batch")),
        P("tp", "batch"),
        P("batch"),
    )
    body = functools.partial(shards, batch=mesh.shape["batch"])
    return jax.shard_map(body, mesh=mesh, in_specs=in_specs, out_specs=out_specs, check_vma=False)
```

time: 1220 us -> 385 us (0.32)
  waiting for transfers between devices: 671 us -> 84.5 us
  matrix products: 245 us -> 0 us
  Pallas kernels: 0 us -> 114 us
  other arithmetic: 109 us -> 20.2 us
  local copies, waits for them, and re-layouts: 92.3 us -> 47.3 us
  starting transfers between devices: 0.67 us -> 42.7 us
  between operations: 16.9 us -> 1.27 us
    reduce_scatter x4 -> x0, waiting for transfers between devices: 546 us -> none  [the longest x1 143 us: shards(): lax.psum_scatter(w_back_grad, 'batch', scatter_dimension=1, tiled=True)]
    dot_general x30 -> x0, matrix products: 229 us -> none  [the longest x4 53 us: masked_scores(): jnp.einsum('qhe,khe->hqk', rows, keys, preferred_element_type=jnp.float32)]
    psum x5 -> x0, waiting for transfers between devices: 116 us -> none  [the longest x2 43.7 us: shards(): summed = lax.psum(partial_out, 'tp')]
    pallas_call x0 -> x17, Pallas kernels: none -> 114 us  [the longest x6 23.2 us: weight_grad(): pl.pallas_call(functools.partial(grad_kernel, parts, group), grid_spec=pl...]
    ppermute x0 -> x35, waiting for transfers between devices: none -> 84.5 us  [the longest x30 84.4 us: swap(): return lax.ppermute(block, ('batch', 'tp'), perm)]
    reduce_sum x17 -> x0, other arithmetic: 53.2 us -> none  [the longest x2 18.1 us: one_block(): total = jnp.sum(expo, -1, keepdims=True)]
    convert_element_type x9 -> x1, other arithmetic: 51.1 us -> 5.45 us  [shards(): layer_out = (middle + (mlp_own + mlp_peer) + back_bias).astype(bf16)]
    ppermute x0 -> x35, starting transfers between devices: none -> 42.7 us  [the longest x30 41.6 us: swap(): return lax.ppermute(block, ('batch', 'tp'), perm)]
  transfers between devices with their start and end apart: 10 -> 35, of which waited for: 10 -> 14; matrix products, arithmetic and copies ran while one was open for 4% -> 6% of each run, Pallas kernels for 0% -> 21%
where the time goes in v1:
time: 385 us; the launch traced here: 384 us
  Pallas kernels  114 us (30%)
  waiting for transfers between devices  84.5 us (22%)
  blocking collectives  74.2 us (19%)
  local copies, waits for them, and re-layouts  47.3 us (12%)
  starting transfers between devices  42.7 us (11%)
  other arithmetic  20.2 us (5%)
    ppermute x30, waiting for transfers between devices, swap(): return lax.ppermute(block, ('batch', 'tp'), perm)  84.4 us
    unnamed x1, blocking collectives  74.2 us
    ppermute x30, starting transfers between devices, swap(): return lax.ppermute(block, ('batch', 'tp'), perm)  41.6 us
    unnamed x127, local copies, waits for them, and re-layouts  39.5 us
    pallas_call x6, Pallas kernels, weight_grad(): pl.pallas_call(functools.partial(grad_kernel, parts, group), grid_spec=pl...  23.2 us
    pallas_call x1, Pallas kernels, attend_back(): pl.pallas_call(attend_back_kernel, grid=(width // PAIR,), in_specs=[pair,...  22 us
    pallas_call x2, Pallas kernels, attend(): pl.pallas_call(functools.partial(attend_kernel, half), grid=(width // PAI...  21.4 us
    pallas_call x2, Pallas kernels, hidden_layer(): pl.pallas_call(hidden_kernel, grid=(per,), in_specs=[glob(dim), loc(dim),...  13.2 us
  transfers between devices with their start and end apart: 35, of which 14 were waited for; matrix products, arithmetic and copies ran while one was open for 6% of the time, Pallas kernels for 21%

profile of v1, /device:TPU:0, one launch (start us, length us, event | category | flops | bytes accessed | tf_op | source)
XLA Modules:
  0.0 383.9 jit_solution(5186550439175533873)
XLA Ops:
  7.4 4.6 %project.1 = (bf16[1216,768]{1,0:T(8,128)(2,1)S(1)}, bf16[1216,384]{1,0:T(8,128)(2,1)S(1)}, bf16[1216,384]{1,0:T(8,128)(2,1)S(1)}, bf16[1216,384]{1,0:T(8,128)(2,1)S(1)}) custom-call(bf16[1216,768]{1,0:T(8,128)(2,1)S(1)} %copy-done.2, f32[1,768]{1,0:T(1,128)S(1)} %reshape.66.gain_ref, f32[1,768]{1,0:T(1,128)S(1)} %reshape.67.shift_ref, ...), custom_call_target="tpu_custom_call" | custom-call | flops 2151677952 | bytes 8306688 | tf_op jit(solution)/shard_map/project/pallas_call | solution.py:74
  13.3 10.4 %attend.2 = (bf16[1216,384]{1,0:T(8,128)(2,1)S(1)}, f32[1216,384]{1,0:T(8,128)}, f32[608,768]{1,0:T(8,128)}) custom-call(bf16[1216,384]{1,0:T(8,128)(2,1)S(1)} %get-tuple-element.58.q_ref, bf16[1216,384]{1,0:T(8,128)(2,1)S(1)} %get-tuple-element.59.k_ref, bf16[1216,384]{1,0:T(8,128)(2,1)S(1)} %get-tuple-element.60.v_ref, s32[1216,1]{1,0:T(8,128)S(1)} %reshape.75.col_ref, ...), custom_call_target="tpu_custom_call" | custom-call | flops 2570059776 | bytes 4669440 | tf_op jit(solution)/shard_map/attend/pallas_call | solution.py:135
  24.3 11.0 %attend.3 = (bf16[1216,384]{1,0:T(8,128)(2,1)S(1)}, f32[1216,384]{1,0:T(8,128)}, f32[608,768]{1,0:T(8,128)}) custom-call(bf16[1216,384]{1,0:T(8,128)(2,1)S(1)} %get-tuple-element.58.q_ref, bf16[1216,384]{1,0:T(8,128)(2,1)S(1)} %get-tuple-element.59.k_ref, ...), custom_call_target="tpu_custom_call", output_to_operand_aliasing={{0}: (6, {}), {1}: (7, {})} | custom-call | flops 2868903936 | bytes 4669440 | tf_op jit(solution)/shard_map/attend/pallas_call | solution.py:135
  39.6 6.7 %hidden_layer.2 = (f32[1216,768]{1,0:T(8,128)S(1)}, bf16[1216,768]{1,0:T(8,128)(2,1)S(1)}, bf16[1216,1536]{1,0:T(8,128)(2,1)}, bf16[1216,1536]{1,0:T(8,128)(2,1)}) custom-call(bf16[1216,768]{1,0:T(8,128)(2,1)S(1)} %copy-done.3, f32[608,768]{1,0:T(8,128)S(1)} %copy-done.23, f32[608,768]{1,0:T(8,128)} %collective-permute-done.1.peer_ref, ...), custom_call_target="tpu_custom_call" | custom-call | flops 1434451968 | bytes 13565952 | tf_op jit(solution)/shard_map/hidden_layer/pallas_call | solution.py:187
  46.3 6.6 %hidden_layer.3 = (f32[1216,768]{1,0:T(8,128)S(1)}, bf16[1216,768]{1,0:T(8,128)(2,1)S(1)}, bf16[1216,1536]{1,0:T(8,128)(2,1)}, bf16[1216,1536]{1,0:T(8,128)(2,1)}) custom-call(bf16[1216,768]{1,0:T(8,128)(2,1)S(1)} %copy-done.3, f32[608,768]{1,0:T(8,128)S(1)} %copy-done.20, ...), custom_call_target="tpu_custom_call", output_to_operand_aliasing={{0}: (8, {}), {1}: (9, {}), {2}: (10, {}), {3}: (11, {})} | custom-call | flops 1434451968 | bytes 13565952 | tf_op jit(solution)/shard_map/hidden_layer/pallas_call | solution.py:187
  54.1 3.4 copy-done.16
  59.0 7.5 %weight_grad.11 = (f32[384,1536]{1,0:T(8,128)S(1)}, f32[384,1536]{1,0:T(8,128)}) custom-call(s32[16]{0:T(128)S(1)} %broadcast_select_fusion.place_ref, bf16[1216,768]{1,0:T(8,128)(2,1)S(1)} %copy-done.26, bf16[1216,1536]{1,0:T(8,128)(2,1)S(1)} %copy-done.16), custom_call_target="tpu_custom_call" | custom-call | flops 2868903936 | bytes 10321920 | tf_op jit(solution)/shard_map/weight_grad/pallas_call | solution.py:461
  74.0 10.0 %hidden_back.1 = (bf16[1216,1536]{1,0:T(8,128)(2,1)S(1)}, f32[1216,768]{1,0:T(8,128)}, f32[1,1536]{1,0:T(1,128)S(1)}, f32[1,768]{1,0:T(1,128)S(1)}) custom-call(bf16[1216,768]{1,0:T(8,128)(2,1)S(1)} %copy-done.27, bf16[1216,1536]{1,0:T(8,128)(2,1)} %get-tuple-element.71.slope_ref, bf16[1536,768]{1,0:T(8,128)(2,1)S(1)} %copy-done.40, ...), custom_call_target="tpu_custom_call" | custom-call | flops 5737807872 | bytes 17793024 | tf_op jit(solution)/shard_map/hidden_back/pallas_call | solution.py:262
  87.9 6.6 %weight_grad.10 = (f32[384,1536]{1,0:T(8,128)S(1)}, f32[384,1536]{1,0:T(8,128)S(1)}) custom-call(s32[16]{0:T(128)S(1)} %broadcast_select_fusion.place_ref, bf16[1216,768]{1,0:T(8,128)(2,1)S(1)} %copy-done.22, bf16[1216,1536]{1,0:T(8,128)(2,1)S(1)} %copy-done.51), custom_call_target="tpu_custom_call" | custom-call | flops 2868903936 | bytes 10321920 | tf_op jit(solution)/shard_map/weight_grad/pallas_call | solution.py:461
  94.7 4.7 %mlp_out.1 = f32[1216,768]{1,0:T(8,128)} custom-call(bf16[1216,1536]{1,0:T(8,128)(2,1)S(1)} %copy-done.17, bf16[1536,768]{1,0:T(8,128)(2,1)S(1)} %copy-done.41), custom_call_target="tpu_custom_call" | custom-call | flops 2868903936 | bytes 9830400 | tf_op jit(solution)/shard_map/mlp_out/pallas_call | solution.py:222
  103.7 32.4 %collective-permute-done.25 = f32[384,1536]{1,0:T(8,128)S(1)} collective-permute-done((f32[384,1536]{1,0:T(8,128)S(1)}, f32[384,1536]{1,0:T(8,128)S(1)}, u32[]{:S(2)}, u32[]{:S(2)}) %collective-permute-start.25) | collective-permute-done | bytes 2359328 | tf_op jit(solution)/shard_map/ppermute | solution.py:511
  147.1 7.3 %collective-permute-done.26 = f32[192,1536]{1,0:T(8,128)} collective-permute-done((f32[192,1536]{1,0:T(8,128)}, f32[192,1536]{1,0:T(8,128)}, u32[]{:S(2)}, u32[]{:S(2)}) %collective-permute-start.26) | collective-permute-done | bytes 1179680 | tf_op jit(solution)/shard_map/ppermute | solution.py:511
  154.4 3.8 %collective-permute-start.34 = (f32[48,1536]{1,0:T(8,128)}, f32[48,1536]{1,0:T(8,128)}, u32[]{:S(2)}, u32[]{:S(2)}) collective-permute-start(f32[48,1536]{1,0:T(8,128)} %get-tuple-element.114), channel_id=1, source_target_pairs={{0,24},{1,25},{2,26},{3,27},{4,28},{5,29},{6,30},{7,31},{8,16},{9,... | collective-permute-start | bytes 884744 | tf_op jit(solution)/shard_map/ppermute | solution.py:511
  161.9 6.7 %middle_back.1 = (f32[1216,768]{1,0:T(8,128)S(1)}, bf16[1216,768]{1,0:T(8,128)(2,1)S(1)}, bf16[1216,384]{1,0:T(8,128)(2,1)S(1)}, f32[8,768]{1,0:T(8,128)S(1)}) custom-call(f32[1216,768]{1,0:T(8,128)S(1)} %copy-done.1, f32[1216,768]{1,0:T(8,128)} %get-tuple-element.72.own_ref, f32[1216,768]{1,0:T(8,128)} %collective-permute-done.3.peer_ref, ...), custom_call_target="tpu_custom_call" | custom-call | flops 717225984 | bytes 20201472 | tf_op jit(solution)/shard_map/middle_back/pallas_call | solution.py:302
  172.6 22.0 %attend_back.1 = (bf16[1216,384]{1,0:T(8,128)(2,1)}, bf16[1216,384]{1,0:T(8,128)(2,1)}, bf16[1216,384]{1,0:T(8,128)(2,1)}, f32[8,384]{1,0:T(8,128)}) custom-call(bf16[1216,384]{1,0:T(8,128)(2,1)} %copy-done.52, bf16[1216,384]{1,0:T(8,128)(2,1)} %copy-done.53, bf16[1216,384]{1,0:T(8,128)(2,1)} %copy-done.54, bf16[1216,384]{1,0:T(8,128)(2,1)} %copy-done.42, ...), custom_call_target="tpu_custom_call" | custom-call | flops 11356078080 | bytes 8404992 | tf_op jit(solution)/shard_map/attend_back/pallas_call | solution.py:368
  204.1 5.5 %add_convert_fusion = bf16[1216,768]{1,0:T(8,128)(2,1)} fusion(f32[1216,768]{1,0:T(8,128)S(1)} %copy-done.1, f32[1216,768]{1,0:T(8,128)} %mlp_out.1, f32[1216,768]{1,0:T(8,128)} %collective-permute-done.2, f32[768]{0:T(1024)S(1)} %copy-done.58), kind=kLoop, calls=%fused_computation | loop fusion | flops 3735552 | bytes 13077504 | tf_op jit(solution)/shard_map/convert_element_type | solution.py:580
  220.6 3.9 %normed_back.1.own_ref = f32[1216,768]{1,0:T(8,128)S(1)} custom-call(bf16[1216,384]{1,0:T(8,128)(2,1)S(1)} %copy-done.11, bf16[1216,384]{1,0:T(8,128)(2,1)S(1)} %copy-done.13, bf16[1216,384]{1,0:T(8,128)(2,1)S(1)} %copy-done.15, bf16[3,768,384]{2,1,0:T(8,128)(2,1)S(1)} %bitcast.27), custom_call_target="tpu_custom_call" | custom-call | flops 2151677952 | bytes 8306688 | tf_op jit(solution)/shard_map/normed_back/pallas_call | solution.py:389
  224.5 3.9 %collective-permute-start.29 = (f32[48,1536]{1,0:T(8,128)S(1)}, f32[48,1536]{1,0:T(8,128)S(1)}, u32[]{:S(2)}, u32[]{:S(2)}) collective-permute-start(f32[48,1536]{1,0:T(8,128)S(1)} %copy-done.56), channel_id=1, source_target_pairs={{0,24},{1,25},{2,26},{3,27},{4,28},{5,29},{6,30},{7,31},{8,16},{9,... | collective-permute-start | bytes 884744 | tf_op jit(solution)/shard_map/ppermute | solution.py:511
  240.0 9.1 %collective-permute-done.5 = f32[384,384]{1,0:T(8,128)S(1)} collective-permute-done((f32[384,384]{1,0:T(8,128)S(1)}, f32[384,384]{1,0:T(8,128)S(1)}, u32[]{:S(2)}, u32[]{:S(2)}) %collective-permute-start.5) | collective-permute-done | bytes 589856 | tf_op jit(solution)/shard_map/ppermute | solution.py:511
  251.8 8.7 %collective-permute-done.10 = f32[384,384]{1,0:T(8,128)S(1)} collective-permute-done((f32[384,384]{1,0:T(8,128)S(1)}, f32[384,384]{1,0:T(8,128)S(1)}, u32[]{:S(2)}, u32[]{:S(2)}) %collective-permute-start.10) | collective-permute-done | bytes 589856 | tf_op jit(solution)/shard_map/ppermute | solution.py:511
  262.1 7.8 %collective-permute-done.15 = f32[384,384]{1,0:T(8,128)S(1)} collective-permute-done((f32[384,384]{1,0:T(8,128)S(1)}, f32[384,384]{1,0:T(8,128)S(1)}, u32[]{:S(2)}, u32[]{:S(2)}) %collective-permute-start.15) | collective-permute-done | bytes 589856 | tf_op jit(solution)/shard_map/ppermute | solution.py:511
  283.4 6.1 %collective-permute-done.13 = f32[48,384]{1,0:T(8,128)S(1)} collective-permute-done((f32[48,384]{1,0:T(8,128)S(1)}, f32[48,384]{1,0:T(8,128)S(1)}, u32[]{:S(2)}, u32[]{:S(2)}) %collective-permute-start.13) | collective-permute-done | bytes 73760 | tf_op jit(solution)/shard_map/ppermute | solution.py:511
  301.6 4.1 %input_back.1 = (bf16[1216,768]{1,0:T(8,128)(2,1)}, f32[8,768]{1,0:T(8,128)S(1)}) custom-call(bf16[1216,768]{1,0:T(8,128)(2,1)S(1)} %copy-done.3, f32[1216,768]{1,0:T(8,128)S(1)} %normed_back.1.own_ref, f32[1216,768]{1,0:T(8,128)S(1)} %collective-permute-done.4.peer_ref, f32[1216,768]{1,0:T(8,128)S(1)} %copy-done.9, f32[1,768]{1,0:T(1,128)S(1)} %reshape.66.gain_ref), custom_call_target="tpu_custom_call" | custom-call | flops 18677760 | bytes 14942208 | tf_op jit(solution)/shard_map/input_back/pallas_call | solution.py:418
  306.0 74.2 %all-reduce = f32[16,432]{1,0:T(8,128)S(1)} all-reduce(f32[16,432]{1,0:T(8,128)S(1)} %concatenate.3), channel_id=2, replica_groups=mesh['batch'=16,'tp'=2] {'batch'}, use_global_device_ids=true, to_apply=%region_0.1.clone | all-reduce | flops 6912 | bytes 55296
  (239 shorter events, 115.7 us)
Async XLA Ops:
  23.8 12.6 %collective-permute-start.1 = (f32[608,768]{1,0:T(8,128)}, f32[608,768]{1,0:T(8,128)}, u32[]{:S(2)}, u32[]{:S(2)}) collective-permute-start(f32[608,768]{1,0:T(8,128)} %get-tuple-element.64.own_ref), channel_id=1, source_target_pairs={{0,1},{1,0},{2,3},{3,2},{4,5},{5,4},{6,7},{7,6},{8,9},{9,8},{10,11... | collective-permute-start | bytes 5603336 | tf_op jit(solution)/shard_map/ppermute | solution.py:534
  36.2 10.0 %collective-permute-start = (f32[608,768]{1,0:T(8,128)}, f32[608,768]{1,0:T(8,128)}, u32[]{:S(2)}, u32[]{:S(2)}) collective-permute-start(f32[608,768]{1,0:T(8,128)} %get-tuple-element.63.own_ref), channel_id=1, source_target_pairs={{0,1},{1,0},{2,3},{3,2},{4,5},{5,4},{6,7},{7,6},{8,9},{9,8},{10,11... | collective-permute-start | bytes 5603336 | tf_op jit(solution)/shard_map/ppermute | solution.py:534
  67.9 31.9 %collective-permute-start.30 = (f32[384,1536]{1,0:T(8,128)}, f32[384,1536]{1,0:T(8,128)S(1)}, u32[]{:S(2)}, u32[]{:S(2)}) collective-permute-start(f32[384,1536]{1,0:T(8,128)} %get-tuple-element.101), channel_id=1, source_target_pairs={{0,2},{1,5},{2,0},{3,7},{4,6},{5,1},{6,4},{7,3},{8,10},{9,13},{10,... | collective-permute-start | bytes 7077896 | tf_op jit(solution)/shard_map/ppermute | solution.py:511
  94.6 41.5 %collective-permute-start.25 = (f32[384,1536]{1,0:T(8,128)S(1)}, f32[384,1536]{1,0:T(8,128)S(1)}, u32[]{:S(2)}, u32[]{:S(2)}) collective-permute-start(f32[384,1536]{1,0:T(8,128)S(1)} %get-tuple-element.99), channel_id=1, source_target_pairs={{0,2},{1,5},{2,0},{3,7},{4,6},{5,1},{6,4},{7,3},{8,10},{9,13},{10,... | collective-permute-start | bytes 7077896 | tf_op jit(solution)/shard_map/ppermute | solution.py:511
  94.6 65.7 %collective-permute-start.3 = (f32[1216,768]{1,0:T(8,128)}, f32[1216,768]{1,0:T(8,128)}, u32[]{:S(2)}, u32[]{:S(2)}) collective-permute-start(f32[1216,768]{1,0:T(8,128)} %get-tuple-element.72.own_ref), channel_id=1, source_target_pairs={{0,1},{1,0},{2,3},{3,2},{4,5},{5,4},{6,7},{7,6},{8,9},{9,8},{10,11... | collective-permute-start | bytes 11206664 | tf_op jit(solution)/shard_map/ppermute | solution.py:534
  99.4 104.1 %collective-permute-start.2 = (f32[1216,768]{1,0:T(8,128)}, f32[1216,768]{1,0:T(8,128)}, u32[]{:S(2)}, u32[]{:S(2)}) collective-permute-start(f32[1216,768]{1,0:T(8,128)} %mlp_out.1), channel_id=1, source_target_pairs={{0,1},{1,0},{2,3},{3,2},{4,5},{5,4},{6,7},{7,6},{8,9},{9,8},{10,11... | collective-permute-start | bytes 11206664 | tf_op jit(solution)/shard_map/ppermute | solution.py:534
  101.7 38.8 %collective-permute-start.31 = (f32[192,1536]{1,0:T(8,128)}, f32[192,1536]{1,0:T(8,128)}, u32[]{:S(2)}, u32[]{:S(2)}) collective-permute-start(f32[192,1536]{1,0:T(8,128)} %get-tuple-element.110), channel_id=1, source_target_pairs={{0,4},{1,3},{2,6},{3,1},{4,0},{5,7},{6,2},{7,5},{8,12},{9,11},{10,... | collective-permute-start | bytes 3538952 | tf_op jit(solution)/shard_map/ppermute | solution.py:511
  137.9 16.5 %collective-permute-start.26 = (f32[192,1536]{1,0:T(8,128)}, f32[192,1536]{1,0:T(8,128)}, u32[]{:S(2)}, u32[]{:S(2)}) collective-permute-start(f32[192,1536]{1,0:T(8,128)} %get-tuple-element.112), channel_id=1, source_target_pairs={{0,4},{1,3},{2,6},{3,1},{4,0},{5,7},{6,2},{7,5},{8,12},{9,11},{10,... | collective-permute-start | bytes 3538952 | tf_op jit(solution)/shard_map/ppermute | solution.py:511
  143.0 81.6 %collective-permute-start.32 = (f32[48,1536]{1,0:T(8,128)}, f32[48,1536]{1,0:T(8,128)}, u32[]{:S(2)}, u32[]{:S(2)}) collective-permute-start(f32[48,1536]{1,0:T(8,128)} %get-tuple-element.113), channel_id=1, source_target_pairs={{0,8},{1,9},{2,10},{3,11},{4,12},{5,13},{6,14},{7,15},{8,0},{9,1},... | collective-permute-start | bytes 884744 | tf_op jit(solution)/shard_map/ppermute | solution.py:511
  144.5 83.9 %collective-permute-start.33 = (f32[48,1536]{1,0:T(8,128)}, f32[48,1536]{1,0:T(8,128)}, u32[]{:S(2)}, u32[]{:S(2)}) collective-permute-start(f32[48,1536]{1,0:T(8,128)} %get-tuple-element.115), channel_id=1, source_target_pairs={{0,16},{1,17},{2,18},{3,19},{4,20},{5,21},{6,22},{7,23},{8,24},{9,... | collective-permute-start | bytes 884744 | tf_op jit(solution)/shard_map/ppermute | solution.py:511
  154.4 75.5 %collective-permute-start.34 = (f32[48,1536]{1,0:T(8,128)}, f32[48,1536]{1,0:T(8,128)}, u32[]{:S(2)}, u32[]{:S(2)}) collective-permute-start(f32[48,1536]{1,0:T(8,128)} %get-tuple-element.114), channel_id=1, source_target_pairs={{0,24},{1,25},{2,26},{3,27},{4,28},{5,29},{6,30},{7,31},{8,16},{9,... | collective-permute-start | bytes 884744 | tf_op jit(solution)/shard_map/ppermute | solution.py:511
  160.4 71.7 %collective-permute-start.27 = (f32[48,1536]{1,0:T(8,128)}, f32[48,1536]{1,0:T(8,128)}, u32[]{:S(2)}, u32[]{:S(2)}) collective-permute-start(f32[48,1536]{1,0:T(8,128)} %get-tuple-element.116), channel_id=1, source_target_pairs={{0,8},{1,9},{2,10},{3,11},{4,12},{5,13},{6,14},{7,15},{8,0},{9,1},... | collective-permute-start | bytes 884744 | tf_op jit(solution)/shard_map/ppermute | solution.py:511
  203.5 29.1 %collective-permute-start.28 = (f32[48,1536]{1,0:T(8,128)}, f32[48,1536]{1,0:T(8,128)}, u32[]{:S(2)}, u32[]{:S(2)}) collective-permute-start(f32[48,1536]{1,0:T(8,128)} %get-tuple-element.118), channel_id=1, source_target_pairs={{0,16},{1,17},{2,18},{3,19},{4,20},{5,21},{6,22},{7,23},{8,24},{9,... | collective-permute-start | bytes 884744 | tf_op jit(solution)/shard_map/ppermute | solution.py:511
  224.5 9.6 %collective-permute-start.29 = (f32[48,1536]{1,0:T(8,128)S(1)}, f32[48,1536]{1,0:T(8,128)S(1)}, u32[]{:S(2)}, u32[]{:S(2)}) collective-permute-start(f32[48,1536]{1,0:T(8,128)S(1)} %copy-done.56), channel_id=1, source_target_pairs={{0,24},{1,25},{2,26},{3,27},{4,28},{5,29},{6,30},{7,31},{8,16},{9,... | collective-permute-start | bytes 884744 | tf_op jit(solution)/shard_map/ppermute | solution.py:511
  228.4 9.9 %collective-permute-start.20 = (f32[384,384]{1,0:T(8,128)S(1)}, f32[384,384]{1,0:T(8,128)S(1)}, u32[]{:S(2)}, u32[]{:S(2)}) collective-permute-start(f32[384,384]{1,0:T(8,128)S(1)} %get-tuple-element.95), channel_id=1, source_target_pairs={{0,2},{1,5},{2,0},{3,7},{4,6},{5,1},{6,4},{7,3},{8,10},{9,13},{10,... | collective-permute-start | bytes 1769480 | tf_op jit(solution)/shard_map/ppermute | solution.py:511
  229.9 71.7 %collective-permute-start.4 = (f32[1216,768]{1,0:T(8,128)S(1)}, f32[1216,768]{1,0:T(8,128)S(1)}, u32[]{:S(2)}, u32[]{:S(2)}) collective-permute-start(f32[1216,768]{1,0:T(8,128)S(1)} %normed_back.1.own_ref), channel_id=1, source_target_pairs={{0,1},{1,0},{2,3},{3,2},{4,5},{5,4},{6,7},{7,6},{8,9},{9,8},{10,11... | collective-permute-start | bytes 11206664 | tf_op jit(solution)/shard_map/ppermute | solution.py:534
  232.0 17.0 %collective-permute-start.5 = (f32[384,384]{1,0:T(8,128)S(1)}, f32[384,384]{1,0:T(8,128)S(1)}, u32[]{:S(2)}, u32[]{:S(2)}) collective-permute-start(f32[384,384]{1,0:T(8,128)S(1)} %copy-done.48), channel_id=1, source_target_pairs={{0,2},{1,5},{2,0},{3,7},{4,6},{5,1},{6,4},{7,3},{8,10},{9,13},{10,... | collective-permute-start | bytes 1769480 | tf_op jit(solution)/shard_map/ppermute | solution.py:511
  232.6 27.8 %collective-permute-start.10 = (f32[384,384]{1,0:T(8,128)S(1)}, f32[384,384]{1,0:T(8,128)S(1)}, u32[]{:S(2)}, u32[]{:S(2)}) collective-permute-start(f32[384,384]{1,0:T(8,128)S(1)} %copy-done.44), channel_id=1, source_target_pairs={{0,2},{1,5},{2,0},{3,7},{4,6},{5,1},{6,4},{7,3},{8,10},{9,13},{10,... | collective-permute-start | bytes 1769480 | tf_op jit(solution)/shard_map/ppermute | solution.py:511
  234.1 35.8 %collective-permute-start.15 = (f32[384,384]{1,0:T(8,128)S(1)}, f32[384,384]{1,0:T(8,128)S(1)}, u32[]{:S(2)}, u32[]{:S(2)}) collective-permute-start(f32[384,384]{1,0:T(8,128)S(1)} %copy-done.46), channel_id=1, source_target_pairs={{0,2},{1,5},{2,0},{3,7},{4,6},{5,1},{6,4},{7,3},{8,10},{9,13},{10,... | collective-permute-start | bytes 1769480 | tf_op jit(solution)/shard_map/ppermute | solution.py:511
  238.4 33.2 %collective-permute-start.21 = (f32[192,384]{1,0:T(8,128)S(1)}, f32[192,384]{1,0:T(8,128)S(1)}, u32[]{:S(2)}, u32[]{:S(2)}) collective-permute-start(f32[192,384]{1,0:T(8,128)S(1)} %get-tuple-element.120), channel_id=1, source_target_pairs={{0,4},{1,3},{2,6},{3,1},{4,0},{5,7},{6,2},{7,5},{8,12},{9,11},{10,... | collective-permute-start | bytes 884744 | tf_op jit(solution)/shard_map/ppermute | solution.py:511
  249.2 22.5 %collective-permute-start.6 = (f32[192,384]{1,0:T(8,128)S(1)}, f32[192,384]{1,0:T(8,128)S(1)}, u32[]{:S(2)}, u32[]{:S(2)}) collective-permute-start(f32[192,384]{1,0:T(8,128)S(1)} %get-tuple-element.122), channel_id=1, source_target_pairs={{0,4},{1,3},{2,6},{3,1},{4,0},{5,7},{6,2},{7,5},{8,12},{9,11},{10,... | collective-permute-start | bytes 884744 | tf_op jit(solution)/shard_map/ppermute | solution.py:511
  260.5 13.3 %collective-permute-start.11 = (f32[192,384]{1,0:T(8,128)S(1)}, f32[192,384]{1,0:T(8,128)S(1)}, u32[]{:S(2)}, u32[]{:S(2)}) collective-permute-start(f32[192,384]{1,0:T(8,128)S(1)} %get-tuple-element.124), channel_id=1, source_target_pairs={{0,4},{1,3},{2,6},{3,1},{4,0},{5,7},{6,2},{7,5},{8,12},{9,11},{10,... | collective-permute-start | bytes 884744 | tf_op jit(solution)/shard_map/ppermute | solution.py:511
  271.6 25.7 %collective-permute-start.22 = (f32[48,384]{1,0:T(8,128)S(1)}, f32[48,384]{1,0:T(8,128)S(1)}, u32[]{:S(2)}, u32[]{:S(2)}) collective-permute-start(f32[48,384]{1,0:T(8,128)S(1)} %get-tuple-element.127), channel_id=1, source_target_pairs={{0,8},{1,9},{2,10},{3,11},{4,12},{5,13},{6,14},{7,15},{8,0},{9,1},... | collective-permute-start | bytes 221192 | tf_op jit(solution)/shard_map/ppermute | solution.py:511
  279.5 10.1 %collective-permute-start.13 = (f32[48,384]{1,0:T(8,128)S(1)}, f32[48,384]{1,0:T(8,128)S(1)}, u32[]{:S(2)}, u32[]{:S(2)}) collective-permute-start(f32[48,384]{1,0:T(8,128)S(1)} %get-tuple-element.135), channel_id=1, source_target_pairs={{0,16},{1,17},{2,18},{3,19},{4,20},{5,21},{6,22},{7,23},{8,24},{9,... | collective-permute-start | bytes 221192 | tf_op jit(solution)/shard_map/ppermute | solution.py:511
  (74 other events, 514.5 us)

commit v2 on v1

--- a/solution.py
+++ b/solution.py
@@ -11,7 +11,9 @@
 PAIR = 2 * HEAD_DIM
 HALF = 608
 TILE = 304
-WINDOWS = ((0, 688), (448, 1216))
+LANES = 384
+VMEM_LIMIT = 63 << 20
+TILES = ((0, 256, 0, 608), (256, 352, 0, 688), (608, 256, 448, 1216), (864, 352, 608, 1216))
 f32 = jnp.float32
 bf16 = jnp.bfloat16
 
@@ -77,31 +79,34 @@
         in_specs=[rows(dim), whole((1, dim)), whole((1, dim)), whole(w3.shape), whole((2, width))],
         out_specs=[rows(dim), rows(width), rows(width), rows(width)],
         out_shape=[jax.ShapeDtypeStruct((tok, dim), bf16), out, out, out],
-        compiler_params=params(32),
+        compiler_params=params(60),
         cost_estimate=cost(2 * tok * dim * 3 * width, tok * (2 * dim + 3 * width) * 2 + w3.size * 2),
         name="project",
     )(tokens, gain, shift, w3, qv_bias)
 
 
 def attend_kernel(half, q_ref, k_ref, v_ref, col_ref, row_ref, w_ref, *refs):
-    o_ref, lse_ref, part_ref, mask_ref = refs[-4:]
-    low, high = WINDOWS[half]
+    o_ref, lse_ref, part_ref, *mask_refs = refs[-5:]
     step = pl.program_id(0)
+    tiles = TILES[2 * half : 2 * half + 2]
 
     @pl.when(step == 0)
     def _():
-        same = col_ref[...] == row_ref[:, low:high]
-        mask_ref[...] = jnp.where(same, 0.0, -1000000000.0)
+        for (start, count, low, high), mask_ref in zip(tiles, mask_refs):
+            at = start - half * HALF
+            same = col_ref[at : at + count, :] == row_ref[:, low:high]
+            mask_ref[...] = jnp.where(same, 0.0, -1000000000.0)
 
     first = lax.broadcasted_iota(jnp.int32, (1, PAIR), 1) < HEAD_DIM
-    keys = k_ref[low:high, :]
-    values = v_ref[low:high, :]
     zero = jnp.zeros((), bf16)
     one = jnp.ones((), bf16)
-    with_ones = (jnp.where(first, values, one), jnp.where(first, one, values))
-    for at in range(0, HALF, TILE):
-        rows = q_ref[at : at + TILE, :]
-        mask = mask_ref[at : at + TILE, :]
+    for tile, ((start, count, low, high), mask_ref) in enumerate(zip(tiles, mask_refs)):
+        at = start - half * HALF
+        rows = q_ref[at : at + count, :]
+        keys = k_ref[low:high, :]
+        values = v_ref[low:high, :]
+        with_ones = (jnp.where(first, values, one), jnp.where(first, one, values))
+        mask = mask_ref[...]
         outs, logs = [], []
         for head in range(2):
             own = jnp.where(first, rows, zero) if head == 0 else jnp.where(first, zero, rows)
@@ -113,25 +118,27 @@
             outs.append(mixed / total)
             logs.append(top + jnp.log(total))
         mixed = jnp.where(first, outs[0], outs[1]).astype(bf16)
-        o_ref[at : at + TILE, :] = mixed
-        lse_ref[at : at + TILE, :] = jnp.where(first, logs[0], logs[1])
+        o_ref[at : at + count, :] = mixed
+        turned = jnp.transpose(jnp.where(first, logs[0], logs[1]))
+        lse_ref[tile, pl.ds(2 * step, 1), 0:count] = turned[0:1, :]
+        lse_ref[tile, pl.ds(2 * step + 1, 1), 0:count] = turned[HEAD_DIM : HEAD_DIM + 1, :]
         part = nn(mixed, w_ref[...])
 
         @pl.when(step == 0)
         def _():
-            part_ref[at : at + TILE, :] = part
+            part_ref[at : at + count, :] = part
 
         @pl.when(step > 0)
         def _():
-            part_ref[at : at + TILE, :] += part
+            part_ref[at : at + count, :] += part
 
 
 def attend(half, q, k, v, ids_col, ids_row, w_out, before=()):
     tok, width = q.shape
     dim = w_out.shape[1]
-    low, high = WINDOWS[half]
     pair_rows = pl.BlockSpec((HALF, PAIR), lambda p: (half, p))
     pair_all = pl.BlockSpec((tok, PAIR), lambda p: (0, p))
+    tiles = TILES[2 * half : 2 * half + 2]
     return pl.pallas_call(
         functools.partial(attend_kernel, half),
         grid=(width // PAIR,),
@@ -144,16 +151,16 @@
             pl.BlockSpec((PAIR, dim), lambda p: (p, 0)),
         ]
         + [pl.BlockSpec(memory_space=pl.ANY)] * len(before),
-        out_specs=[pair_rows, pair_rows, whole((HALF, dim))],
+        out_specs=[pair_rows, whole((2, 8, LANES)), whole((HALF, dim))],
         out_shape=[
             jax.ShapeDtypeStruct((tok, width), bf16),
-            jax.ShapeDtypeStruct((tok, width), f32),
+            jax.ShapeDtypeStruct((2, 8, LANES), f32),
             jax.ShapeDtypeStruct((HALF, dim), f32),
         ],
-        scratch_shapes=[pltpu.VMEM((HALF, high - low), f32)],
+        scratch_shapes=[pltpu.VMEM((count, high - low), f32) for _, count, low, high in tiles],
         input_output_aliases={6 + i: i for i in range(len(before))},
-        compiler_params=params(48),
-        cost_estimate=cost(16 * HALF * (high - low) * width, tok * width * 6 + HALF * dim * 4),
+        compiler_params=params(60),
+        cost_estimate=cost(16 * HALF * 650 * width, tok * width * 6 + HALF * dim * 4),
         name="attend",
     )(q, k, v, ids_col, ids_row, w_out, *before)
 
@@ -206,7 +213,7 @@
             jax.ShapeDtypeStruct((tok, width), bf16),
         ],
         input_output_aliases={8 + i: i for i in range(len(before))},
-        compiler_params=params(40),
+        compiler_params=params(60),
         cost_estimate=cost(2 * HALF * dim * width, HALF * (dim * 16 + width * 4) + w_in.size * 2, HALF * width),
         name="hidden_layer",
     )(tokens, own, peer, out_bias, gain, shift, w_in, in_bias, *before)
@@ -225,7 +232,7 @@
         in_specs=[pl.BlockSpec((TILE, depth), lambda i: (i, 0)), whole(b.shape)],
         out_specs=pl.BlockSpec((TILE, width), lambda i: (i, 0)),
         out_shape=jax.ShapeDtypeStruct((tok, width), f32),
-        compiler_params=params(32),
+        compiler_params=params(60),
         cost_estimate=cost(2 * tok * depth * width, tok * (depth * 2 + width * 4) + b.size * 2),
         name="mlp_out",
     )(a, b)
@@ -270,7 +277,7 @@
             jax.ShapeDtypeStruct((1, width), f32),
             jax.ShapeDtypeStruct((1, dim), f32),
         ],
-        compiler_params=params(40),
+        compiler_params=params(60),
         cost_estimate=cost(4 * tok * dim * width, tok * (dim * 6 + width * 4) + w_in.size * 4),
         name="hidden_back",
     )(cotangent, slope, w_back, w_in)
@@ -310,72 +317,87 @@
             jax.ShapeDtypeStruct((tok, width), bf16),
             jax.ShapeDtypeStruct((8, dim), f32),
         ],
-        compiler_params=params(32),
+        compiler_params=params(60),
         cost_estimate=cost(2 * tok * dim * width, tok * (dim * 20 + width * 2) + w_out.size * 2),
         name="middle_back",
     )(middle, own, peer, cotangent, gain, w_out)
 
 
-def attend_back_kernel(q_ref, k_ref, v_ref, do_ref, lse_ref, col_ref, row_ref, dq_ref, dk_ref, dv_ref, sum_ref, acc_k, acc_v):
+def attend_back_tile(tile, keys, values, rows, grads, mask, lse_rows):
     first = lax.broadcasted_iota(jnp.int32, (1, PAIR), 1) < HEAD_DIM
     zero = jnp.zeros((), bf16)
-    for half in range(2):
-        low, high = WINDOWS[half]
-        span = slice(half * HALF, half * HALF + HALF)
-        rows = q_ref[span, :]
-        grads = do_ref[span, :]
-        keys = k_ref[low:high, :]
-        values = v_ref[low:high, :]
-        logs = jnp.transpose(lse_ref[span, :])
+    parts = []
+    for head in range(2):
+        pick = lambda a: jnp.where(first, a, zero) if head == 0 else jnp.where(first, zero, a)
+        probs = jnp.exp(nt(keys, pick(rows)) + mask - lse_rows[head])
+        back = nt(values, pick(grads))
+        inner = jnp.sum(probs * back, 0, keepdims=True)
+        slant = (probs * (back - inner)).astype(bf16)
+        dv = nn(probs.astype(bf16), grads)
+        dk = nn(slant, rows)
+        dq = tn(slant, keys)
+        parts.append((dq, dk, dv))
+    dq, dk, dv = (jnp.where(first, a, b) for a, b in zip(*parts))
+    return (dq * HEAD_DIM ** (-0.5)).astype(bf16), dk, dv
+
+
+def attend_back_pair(q, k, v, do, lse, col_ref, row_ref, put_dq, acc_k, acc_v):
+    total = None
+    for tile, (start, count, low, high) in enumerate(TILES):
+        span = slice(start, start + count)
         mask = jnp.where(col_ref[low:high, :] == row_ref[:, span], 0.0, -1000000000.0)
-        parts = []
-        for head in range(2):
-            pick = lambda a: jnp.where(first, a, zero) if head == 0 else jnp.where(first, zero, a)
-            lse = logs[head * HEAD_DIM : head * HEAD_DIM + 1, :]
-            probs = jnp.exp(nt(keys, pick(rows)) + mask - lse)
-            back = nt(values, pick(grads))
-            inner = jnp.sum(probs * back, 0, keepdims=True)
-            slant = (probs * (back - inner)).astype(bf16)
-            dv = nn(probs.astype(bf16), grads)
-            dk = nn(slant, rows)
-            dq = tn(slant, keys)
-            parts.append((dq, dk, dv))
-        dq, dk, dv = (jnp.where(first, a, b) for a, b in zip(*parts))
-        dq = (dq * HEAD_DIM ** (-0.5)).astype(bf16)
-        dq_ref[span, :] = dq
+        dq, dk, dv = attend_back_tile(
+            tile, k(slice(low, high)), v(slice(low, high)), q(span), do(span), mask, lse(tile, count)
+        )
+        put_dq(span, dq)
         top = jnp.sum(dq.astype(f32), 0, keepdims=True)
-        if half == 0:
-            sum_ref[...] = jnp.zeros_like(sum_ref)
-            acc_k[low:high, :] = dk
-            acc_v[low:high, :] = dv
-        else:
-            edge = WINDOWS[0][1]
-            acc_k[low:edge, :] += dk[: edge - low]
-            acc_v[low:edge, :] += dv[: edge - low]
-            acc_k[edge:high, :] = dk[edge - low :]
-            acc_v[edge:high, :] = dv[edge - low :]
-        sum_ref[0:1, :] += top
+        total = top if total is None else total + top
+        edge = 0 if tile == 0 else TILES[tile - 1][3]
+        for acc, part in ((acc_k, dk), (acc_v, dv)):
+            if edge > low:
+                acc[low:edge, :] += part[: edge - low]
+            if edge < high:
+                acc[edge:high, :] = part[max(edge - low, 0) :]
+    return total
+
+
+def attend_back_kernel(q_ref, k_ref, v_ref, do_ref, lse_a, lse_b, col_ref, row_ref, dq_ref, dk_ref, dv_ref, sum_ref, acc_k, acc_v):
+    step = pl.program_id(0)
+
+    def lse(tile, count):
+        ref = lse_a if tile < 2 else lse_b
+        return [ref[tile % 2, pl.ds(2 * step + head, 1), 0:count] for head in range(2)]
+
+    def put_dq(span, value):
+        dq_ref[span, :] = value
+
+    take = lambda ref: lambda span: ref[span, :]
+    total = attend_back_pair(
+        take(q_ref), take(k_ref), take(v_ref), take(do_ref), lse, col_ref, row_ref, put_dq, acc_k, acc_v
+    )
     dk_ref[...] = acc_k[...].astype(bf16)
     dv = acc_v[...].astype(bf16)
     dv_ref[...] = dv
+    sum_ref[...] = jnp.zeros_like(sum_ref)
+    sum_ref[0:1, :] = total
     sum_ref[1:2, :] = jnp.sum(dv.astype(f32), 0, keepdims=True)
 
 
-def attend_back(q, k, v, do, lse, ids_col, ids_row):
+def attend_back(q, k, v, do, lse_a, lse_b, ids_col, ids_row):
     tok, width = q.shape
     pair = pl.BlockSpec((tok, PAIR), lambda p: (0, p))
     out = jax.ShapeDtypeStruct((tok, width), bf16)
     return pl.pallas_call(
         attend_back_kernel,
         grid=(width // PAIR,),
-        in_specs=[pair, pair, pair, pair, pair, whole((tok, 1)), whole((1, tok))],
+        in_specs=[pair, pair, pair, pair, whole(lse_a.shape), whole(lse_b.shape), whole((tok, 1)), whole((1, tok))],
         out_specs=[pair, pair, pair, pl.BlockSpec((8, PAIR), lambda p: (0, p))],
         out_shape=[out, out, out, jax.ShapeDtypeStruct((8, width), f32)],
         scratch_shapes=[pltpu.VMEM((tok, PAIR), f32), pltpu.VMEM((tok, PAIR), f32)],
-        compiler_params=params(56),
+        compiler_params=params(60),
         cost_estimate=cost(4 * 10 * tok * HALF * width, tok * width * 18),
         name="attend_back",
-    )(q, k, v, do, lse, ids_col, ids_row)
+    )(q, k, v, do, lse_a, lse_b, ids_col, ids_row)
 
 
 def normed_back_kernel(dq_ref, dk_ref, dv_ref, w_ref, o_ref):
@@ -392,7 +414,7 @@
         in_specs=[rows(width), rows(width), rows(width), whole(w3.shape)],
         out_specs=rows(dim),
         out_shape=jax.ShapeDtypeStruct((tok, dim), f32),
-        compiler_params=params(32),
+        compiler_params=params(60),
         cost_estimate=cost(6 * tok * dim * width, tok * (dim * 4 + width * 6) + w3.size * 2),
         name="normed_back",
     )(dq, dk, dv, w3)
@@ -421,7 +443,7 @@
         in_specs=[rows, rows, rows, rows, whole((1, dim))],
         out_specs=[rows, whole((8, dim))],
         out_shape=[jax.ShapeDtypeStruct((tok, dim), bf16), jax.ShapeDtypeStruct((8, dim), f32)],
-        compiler_params=params(32),
+        compiler_params=params(60),
         cost_estimate=cost(20 * tok * dim, tok * dim * 16),
         name="input_back",
     )(tokens, own, peer, dh, gain)
@@ -471,7 +493,7 @@
             scratch_shapes=[pltpu.VMEM((dim, tok), bf16)],
         ),
         out_shape=[jax.ShapeDtypeStruct((rows, width), f32)] * parts,
-        compiler_params=params(40),
+        compiler_params=params(60),
         cost_estimate=cost(2 * tok * dim * width, tok * (dim + width) * 2 + dim * width * 4),
         name="weight_grad",
     )(place, a, b)
@@ -532,6 +554,434 @@
 
 def other_core(values):
     return lax.ppermute(values, "tp", [(0, 1), (1, 0)])
+
+
+COUNT = 12
+SLOTS = 9
+STEPS = 4
+
+
+class Route:
+    def __init__(self):
+        self.me = lax.axis_index("batch")
+        self.core = lax.axis_index("tp")
+        self.bits = {s: lax.rem(self.me // s, 2) for s in (1, 2, 4, 8)}
+        near = {s: self.me + s * (1 - 2 * self.bits[s]) for s in (1, 2, 4, 8)}
+        core = self.core
+        side = near[1] * (1 - core) + near[2] * core
+        other = near[2] * (1 - core) + near[1] * core
+        self.plain = (side, other, near[4], near[8])
+        self.turned = (near[4], side, other, near[8])
+        self.plain_weight = {1: 8 - 4 * core, 2: 4 + 4 * core, 4: 2, 8: 1}
+        self.turned_weight = {4: 8, 1: 4 - 2 * core, 2: 2 + 2 * core, 8: 1}
+
+    def kind(self, chunk):
+        return lax.rem(chunk, 3) // 2
+
+    def partner(self, chunk, step):
+        kind = self.kind(chunk)
+        return self.plain[step] + kind * (self.turned[step] - self.plain[step])
+
+    def places(self, chunk):
+        kind = self.kind(chunk)
+        terms = {}
+        for s in (1, 2, 4, 8):
+            weight = self.plain_weight[s] + kind * (self.turned_weight[s] - self.plain_weight[s])
+            terms[s] = (self.bits[s] * weight, (1 - self.bits[s]) * weight)
+        return [sum(terms[s][(g // s) % 2] for s in (1, 2, 4, 8)) for g in range(16)]
+
+
+def tail_kernel(
+    g_h, hid_h, slope_h, n2_h, mid_h, wi_h, wb_h, wo_h, w3_h, q_h, k_h, v_h, o_h, n1_h, tok_h,
+    lse_a, lse_b, col_ref, row_ref, gain1_ref, gain2_ref, bb_ref,
+    layer_h, input_h, grads_h, sums_ref,
+    buf_h, buf_d, buf_n, buf_g, buf_t, buf_m, own, peer, wi, wb, wo, stage, acc_k, acc_v,
+    chunks, recv0, recv1, recv2, recv3, sums_in,
+    load_sem, stage_sem, send_sem, recv_sem, grad_sem, swap_send, swap_recv, sums_send, sums_recv, put_sem, free_sem,
+):
+    mesh_id = pl.DeviceIdType.MESH
+    route = Route()
+    me, core = route.me, route.core
+    tok, dim = buf_g.shape
+    width = buf_h.shape[1]
+    third = q_h.shape[1]
+    tiles = tok // TILE
+    recvs = (recv0, recv1, recv2, recv3)
+
+    barrier = pltpu.get_barrier_semaphore()
+    for other in route.plain:
+        pl.semaphore_signal(barrier, inc=1, device_id=(other, core), device_id_type=mesh_id)
+    pl.semaphore_signal(barrier, inc=1, device_id=(me, 1 - core), device_id_type=mesh_id)
+
+    def load(source, target, at):
+        return pltpu.make_async_copy(source, target, load_sem.at[at])
+
+    first_loads = [
+        load(g_h, buf_g, 0),
+        load(hid_h, buf_h, 1),
+        load(wb_h, wb, 2),
+        load(slope_h, buf_d, 3),
+        load(wi_h, wi, 4),
+        load(n2_h, buf_n, 5),
+        load(mid_h, buf_m, 6),
+        load(wo_h, wo, 7),
+    ]
+    for item in first_loads:
+        item.start()
+
+
+    def slot_of(chunk):
+        return lax.rem(chunk, SLOTS)
+
+    def hop(chunk, step):
+        half = 8 >> step
+        return pltpu.make_async_remote_copy(
+            src_ref=chunks.at[slot_of(chunk), pl.ds(half, half)],
+            dst_ref=recvs[step].at[chunk],
+            send_sem=send_sem.at[step, chunk],
+            recv_sem=recv_sem.at[step, chunk],
+            device_id=(route.partner(chunk, step), core),
+            device_id_type=mesh_id,
+        )
+
+    def deliver(chunk):
+        return pltpu.make_async_copy(chunks.at[slot_of(chunk), 0], grads_h.at[chunk], grad_sem.at[chunk])
+
+    def finish(chunk, step):
+        got = hop(chunk, step)
+        got.wait_send()
+        got.wait_recv()
+        slot = slot_of(chunk)
+
+        def add(g, carry):
+            chunks[slot, g] += recvs[step][chunk, g]
+            return carry
+
+        lax.fori_loop(0, 8 >> step, add, 0)
+        if step < STEPS - 1:
+            hop(chunk, step + 1).start()
+        else:
+            deliver(chunk).start()
+
+    def tick(at, known=True):
+        for step in range(STEPS - 1, -1, -1):
+            if not known or 0 <= at - step < COUNT:
+                finish(at - step, step)
+
+    def gradient(chunk, right):
+        places = route.places(chunk)
+        slot = slot_of(chunk)
+        total = nn(buf_t[...], right)
+        rows = dim // 16
+        for g in range(16):
+            chunks[slot, places[g]] = total[g * rows : (g + 1) * rows, :]
+
+    def turn(source):
+        def body(i, carry):
+            at = pl.multiple_of(i * PAIR, PAIR)
+            buf_t[pl.ds(at, PAIR), :] = jnp.transpose(source[:, pl.ds(at, PAIR)])
+            return carry
+
+        lax.fori_loop(0, dim // PAIR, body, 0)
+
+    def columns(ref, at):
+        return ref[:, pl.ds(pl.multiple_of(at, PAIR), LANES)]
+
+    def rows_of(i):
+        return pl.ds(pl.multiple_of(i * TILE, TILE), TILE)
+
+
+    def swap(turn_at, i):
+        return pltpu.make_async_remote_copy(
+            src_ref=own.at[rows_of(i)],
+            dst_ref=peer.at[rows_of(i)],
+            send_sem=swap_send.at[turn_at, i],
+            recv_sem=swap_recv.at[turn_at, i],
+            device_id=(me, 1 - core),
+            device_id_type=mesh_id,
+        )
+
+    def swapped(turn_at, i):
+        got = swap(turn_at, i)
+        got.wait_send()
+        got.wait_recv()
+        return own[rows_of(i), :] + peer[rows_of(i), :]
+
+    def peer_is_free():
+        pl.semaphore_signal(free_sem, inc=1, device_id=(me, 1 - core), device_id_type=mesh_id)
+
+
+    first_loads[0].wait()
+    turn(buf_g)
+    pl.semaphore_wait(barrier, STEPS + 1)
+    first_loads[1].wait()
+    for chunk in range(1):
+
+        def body(i, carry):
+            gradient(i, columns(buf_h, i * LANES))
+            hop(i, 0).start()
+            return carry
+
+        lax.fori_loop(0, 4, body, 0)
+
+
+    sums_ref[...] = jnp.zeros_like(sums_ref)
+    for item in first_loads[2:5]:
+        item.wait()
+
+    def body(i, carry):
+        grad = buf_g[rows_of(i), :]
+        for at in range(0, width, 512):
+            back = nt(grad, wb[at : at + 512, :])
+            du = (back * buf_d[rows_of(i), at : at + 512].astype(f32)).astype(bf16)
+            buf_d[rows_of(i), at : at + 512] = du
+            sums_ref[4:5, at : at + 512] += jnp.sum(du.astype(f32), 0, keepdims=True)
+        own[rows_of(i), :] = nt(buf_d[rows_of(i), :], wi[...])
+        swap(0, i).start()
+        sums_ref[2:3, dim : 2 * dim] += jnp.sum(grad.astype(f32), 0, keepdims=True)
+        return carry
+
+    lax.fori_loop(0, tiles, body, 0)
+
+
+    first_loads[5].wait()
+    turn(buf_n)
+    late_load = [load(w3_h.at[c], wi.at[:, pl.ds(c * third, third)], 8 + c) for c in range(3)]
+    for item in late_load:
+        item.start()
+
+    def body(i, carry):
+        gradient(4 + i, columns(buf_d, i * LANES))
+        return carry
+
+    lax.fori_loop(0, 2, body, 0)
+    hop(4, 0).start()
+    hop(5, 0).start()
+    tick(0)
+
+    def body(i, carry):
+        gradient(6 + i, columns(buf_d, i * LANES + 2 * LANES))
+        return carry
+
+    lax.fori_loop(0, 2, body, 0)
+    hop(6, 0).start()
+    tick(1)
+    hop(7, 0).start()
+
+
+    first_loads[6].wait()
+    first_loads[7].wait()
+
+    def body(i, carry):
+        grad = swapped(0, i)
+        unit, inv = standardize(buf_m[rows_of(i), :])
+        dh = buf_g[rows_of(i), :].astype(f32) + norm_back(unit, inv, gain2_ref[...], grad)
+        buf_m[rows_of(i), :] = dh
+        dr = dh.astype(bf16)
+        buf_n[rows_of(i), :] = dr
+        buf_d[rows_of(i), 0:third] = nt(dr, wo[...]).astype(bf16)
+        sums_ref[1:2, dim : 2 * dim] += jnp.sum(grad * unit, 0, keepdims=True)
+        sums_ref[2:3, 0:dim] += jnp.sum(grad, 0, keepdims=True)
+        sums_ref[1:2, 0:dim] += jnp.sum(dr.astype(f32), 0, keepdims=True)
+        return carry
+
+    lax.fori_loop(0, tiles, body, 0)
+    peer_is_free()
+    tick(2)
+
+
+    def fetch(i):
+        return pltpu.make_async_copy(mid_h.at[rows_of(i)], stage.at[lax.rem(i, 2)], stage_sem.at[lax.rem(i, 2)])
+
+    fetch(0).start()
+    turn(buf_n)
+    n1_load = load(n1_h, buf_n, 11)
+    n1_load.start()
+    pl.semaphore_wait(free_sem, 1)
+
+    def body(i, carry):
+        own[rows_of(i), :] = nn(buf_h[rows_of(i), :], wb[...])
+        swap(1, i).start()
+        return carry
+
+    lax.fori_loop(0, tiles, body, 0)
+    heads_load = [load(ref, buf_h.at[:, pl.ds(c * third, third)], 12 + c) for c, ref in enumerate((q_h, k_h, v_h, o_h))]
+    for item in heads_load:
+        item.start()
+
+    def body(i, carry):
+        @pl.when(i + 1 < tiles)
+        def _():
+            fetch(i + 1).start()
+
+        fetch(i).wait()
+        buf_g[rows_of(i), :] = (stage[lax.rem(i, 2)] + swapped(1, i) + bb_ref[...]).astype(bf16)
+        return carry
+
+    lax.fori_loop(0, tiles, body, 0)
+    peer_is_free()
+    layer_put = pltpu.make_async_copy(buf_g, layer_h, put_sem.at[0])
+    layer_put.start()
+
+
+    for item in heads_load:
+        item.wait()
+    gradient(8, buf_h[:, 3 * third : 4 * third])
+    tick(3)
+    hop(8, 0).start()
+    layer_put.wait()
+    tok_load = load(tok_h, buf_g, 16)
+    tok_load.start()
+
+
+    def body(p, carry):
+        def take(ref, block):
+            at = pl.multiple_of(block * third + p * PAIR, PAIR)
+            return lambda span: ref[span, pl.ds(at, PAIR)]
+
+        def put(block):
+            at = pl.multiple_of(block * third + p * PAIR, PAIR)
+
+            def store(span, value):
+                buf_d[span, pl.ds(at, PAIR)] = value
+
+            return store
+
+        def lse(tile, count):
+            ref = lse_a if tile < 2 else lse_b
+            return [ref[tile % 2, pl.ds(2 * p + head, 1), 0:count] for head in range(2)]
+
+        total = attend_back_pair(
+            take(buf_h, 0), take(buf_h, 1), take(buf_h, 2), take(buf_d, 0), lse, col_ref, row_ref, put(1), acc_k, acc_v
+        )
+        put(2)(slice(0, tok), acc_k[...].astype(bf16))
+        dv = acc_v[...].astype(bf16)
+        put(3)(slice(0, tok), dv)
+        lane = pl.multiple_of(p * PAIR, PAIR)
+        sums_ref[3:4, pl.ds(lane, PAIR)] = total
+        sums_ref[3:4, pl.ds(pl.multiple_of(third + p * PAIR, PAIR), PAIR)] = jnp.sum(dv.astype(f32), 0, keepdims=True)
+        tick(4 + p, known=False)
+        return carry
+
+    lax.fori_loop(0, third // PAIR, body, 0)
+
+
+    for item in late_load:
+        item.wait()
+    pl.semaphore_wait(free_sem, 1)
+
+    def body(i, carry):
+        own[rows_of(i), :] = nt(buf_d[rows_of(i), third : 4 * third], wi[:, 0 : 3 * third])
+        swap(2, i).start()
+        return carry
+
+    lax.fori_loop(0, tiles, body, 0)
+    n1_load.wait()
+    turn(buf_n)
+    for chunk in range(COUNT - SLOTS):
+        deliver(chunk).wait()
+
+    def body(i, carry):
+        gradient(9 + i, columns(buf_d, i * LANES + third))
+        hop(9 + i, 0).start()
+        return carry
+
+    lax.fori_loop(0, 3, body, 0)
+    tick(7)
+
+
+    tok_load.wait()
+
+    def body(i, carry):
+        grad = swapped(2, i)
+        unit, inv = standardize(buf_g[rows_of(i), :].astype(f32))
+        buf_g[rows_of(i), :] = (buf_m[rows_of(i), :] + norm_back(unit, inv, gain1_ref[...], grad)).astype(bf16)
+        sums_ref[0:1, 0:dim] += jnp.sum(grad * unit, 0, keepdims=True)
+        sums_ref[0:1, dim : 2 * dim] += jnp.sum(grad, 0, keepdims=True)
+        return carry
+
+    lax.fori_loop(0, tiles, body, 0)
+    input_put = pltpu.make_async_copy(buf_g, input_h, put_sem.at[1])
+    input_put.start()
+
+
+    def whole_hop(step):
+        return pltpu.make_async_remote_copy(
+            src_ref=sums_ref,
+            dst_ref=sums_in.at[step],
+            send_sem=sums_send.at[step],
+            recv_sem=sums_recv.at[step],
+            device_id=(route.plain[step], core),
+            device_id_type=mesh_id,
+        )
+
+    for step in range(STEPS):
+        whole_hop(step).start()
+        tick(8 + step)
+        whole_hop(step).wait()
+        sums_ref[...] += sums_in[step]
+    for at in range(8 + STEPS, COUNT + STEPS - 1):
+        tick(at)
+    for chunk in range(COUNT - SLOTS, COUNT):
+        deliver(chunk).wait()
+    input_put.wait()
+
+
+def tail(g, hid, slope, n2, mid, wi, wb, wo, w3, q, k, v, o, n1, tokens, lse_a, lse_b, col, row, gain1, gain2, bb):
+    tok, dim = g.shape
+    width = hid.shape[1]
+    third = q.shape[1]
+    rows = dim // 16
+    hbm = pl.BlockSpec(memory_space=pl.ANY)
+    vmem = pl.BlockSpec(memory_space=pltpu.VMEM)
+    dma = pltpu.SemaphoreType.DMA
+    return pl.pallas_call(
+        tail_kernel,
+        in_specs=[hbm] * 15 + [vmem] * 7,
+        out_specs=[hbm, hbm, hbm, vmem],
+        out_shape=[
+            jax.ShapeDtypeStruct((tok, dim), bf16),
+            jax.ShapeDtypeStruct((tok, dim), bf16),
+            jax.ShapeDtypeStruct((COUNT, rows, LANES), f32),
+            jax.ShapeDtypeStruct((8, width), f32),
+        ],
+        scratch_shapes=[
+            pltpu.VMEM((tok, width), bf16),
+            pltpu.VMEM((tok, width), bf16),
+            pltpu.VMEM((tok, dim), bf16),
+            pltpu.VMEM((tok, dim), bf16),
+            pltpu.VMEM((dim, tok), bf16),
+            pltpu.VMEM((tok, dim), f32),
+            pltpu.VMEM((tok, dim), f32),
+            pltpu.VMEM((tok, dim), f32),
+            pltpu.VMEM((dim, width), bf16),
+            pltpu.VMEM((width, dim), bf16),
+            pltpu.VMEM((third, dim), bf16),
+            pltpu.VMEM((2, TILE, dim), f32),
+            pltpu.VMEM((tok, PAIR), f32),
+            pltpu.VMEM((tok, PAIR), f32),
+            pltpu.VMEM((SLOTS, 16, rows, LANES), f32),
+            pltpu.VMEM((COUNT, 8, rows, LANES), f32),
+            pltpu.VMEM((COUNT, 4, rows, LANES), f32),
+            pltpu.VMEM((COUNT, 2, rows, LANES), f32),
+            pltpu.VMEM((COUNT, 1, rows, LANES), f32),
+            pltpu.VMEM((STEPS, 8, width), f32),
+            dma((17,)),
+            dma((2,)),
+            dma((STEPS, COUNT)),
+            dma((STEPS, COUNT)),
+            dma((COUNT,)),
+            dma((3, tok // TILE)),
+            dma((3, tok // TILE)),
+            dma((STEPS,)),
+            dma((STEPS,)),
+            dma((2,)),
+            pltpu.SemaphoreType.REGULAR,
+        ],
+        compiler_params=pltpu.CompilerParams(vmem_limit_bytes=VMEM_LIMIT, collective_id=0, has_side_effects=True),
+        cost_estimate=cost(24e9, 40e6),
+        name="tail",
+    )(g, hid, slope, n2, mid, wi, wb, wo, w3, q, k, v, o, n1, tokens, lse_a, lse_b, col, row, gain1, gain2, bb)
 
 
 def shards(
@@ -560,41 +1010,55 @@
     parts = exchange.first_parts()
 
     normed, q, k, v = project(tokens, row(norm1_gain), row(norm1_shift), w3, qv_bias)
-    mixed, lse, part_a = attend(0, q, k, v, ids_col, ids_row, w_out)
+    mixed, lse_a, part_a = attend(0, q, k, v, ids_col, ids_row, w_out)
     peer_a = other_core(part_a)
-    mixed, lse, part_b = attend(1, q, k, v, ids_col, ids_row, w_out, (mixed, lse))
+    mixed, lse_b, part_b = attend(1, q, k, v, ids_col, ids_row, w_out, (mixed,))
     peer_b = other_core(part_b)
     mlp = (row(out_bias), row(norm2_gain), row(norm2_shift), w_in, row(in_bias))
     state = hidden_layer(0, tokens, part_a, peer_a, *mlp)
     state = hidden_layer(1, tokens, part_b, peer_b, *mlp, before=tuple(state))
     middle, normed_two, hidden, slope = state
 
-    back_parts = weight_grad(parts, exchange.place, cotangent, hidden)
-    du, dn2, in_bias_sum, back_bias_sum = hidden_back(cotangent, slope, w_back, w_in)
-    dn2_peer = other_core(dn2)
-    in_parts = weight_grad(parts, exchange.place, normed_two, du)
-    mlp_own = rows_matmul(hidden, w_back)
-    mlp_peer = other_core(mlp_own)
-    dh, dr, do, middle_sums = middle_back(middle, dn2, dn2_peer, cotangent, row(norm2_gain), w_out)
-    out_parts = weight_grad(parts, exchange.place, dr, mixed)
-    layer_out = (middle + (mlp_own + mlp_peer) + back_bias).astype(bf16)
-    dq, dk, dv, qv_sums = attend_back(q, k, v, do, lse, ids_col, ids_row)
-    q_parts = weight_grad(parts, exchange.place, normed, dq)
-    k_parts = weight_grad(parts, exchange.place, normed, dk)
-    v_parts = weight_grad(parts, exchange.place, normed, dv)
-    dn1 = normed_back(dq, dk, dv, w3)
-    dn1_peer = other_core(dn1)
-    tokens_grad, input_sums = input_back(tokens, dn1, dn1_peer, dh, row(norm1_gain))
-
-    w_back_grad = jnp.transpose(exchange.reduce(back_parts))
-    w_in_grad = exchange.reduce(in_parts)
-    w_out_grad = jnp.transpose(exchange.reduce(out_parts))
-    w_qkv_grad = jnp.stack([exchange.reduce(p) for p in (q_parts, k_parts, v_parts)], 1)
-
-    pieces = [input_sums[0], input_sums[1], middle_sums[2], middle_sums[0], middle_sums[1], back_bias_sum[0]]
-    pieces += [qv_sums[0], qv_sums[1], in_bias_sum[0]]
-    packed = jnp.concatenate([p.reshape(batch, -1) for p in pieces], 1)
-    vectors = lax.psum_scatter(packed, "batch", scatter_dimension=0, tiled=True)[0]
+    if batch == 16:
+        layer_out, tokens_grad, grads, sums = tail(
+            cotangent, hidden, slope, normed_two, middle, w_in, w_back, w_out, w3, q, k, v, mixed, normed, tokens,
+            lse_a, lse_b, ids_col, ids_row, row(norm1_gain), row(norm2_gain), row(back_bias),
+        )
+        wide = lambda part: jnp.transpose(part, (0, 2, 1)).reshape(-1, dim // batch)
+        w_back_grad = wide(grads[0:4])
+        w_in_grad = jnp.transpose(grads[4:8], (1, 0, 2)).reshape(dim // batch, -1)
+        w_out_grad = wide(grads[8:9])
+        w_qkv_grad = jnp.transpose(grads[9:12], (1, 0, 2))
+        third = q.shape[1]
+        pieces = [sums[0, :dim], sums[0, dim:], sums[1, :dim], sums[1, dim:], sums[2, :dim], sums[2, dim:]]
+        pieces += [sums[3, :third], sums[3, third : 2 * third], sums[4]]
+        packed = jnp.concatenate([p.reshape(batch, -1) for p in pieces], 1)
+        vectors = lax.dynamic_index_in_dim(packed, lax.axis_index("batch"), 0, keepdims=False)
+    else:
+        back_parts = weight_grad(parts, exchange.place, cotangent, hidden)
+        du, dn2, in_bias_sum, back_bias_sum = hidden_back(cotangent, slope, w_back, w_in)
+        dn2_peer = other_core(dn2)
+        in_parts = weight_grad(parts, exchange.place, normed_two, du)
+        mlp_own = rows_matmul(hidden, w_back)
+        mlp_peer = other_core(mlp_own)
+        dh, dr, do, middle_sums = middle_back(middle, dn2, dn2_peer, cotangent, row(norm2_gain), w_out)
+        out_parts = weight_grad(parts, exchange.place, dr, mixed)
+        layer_out = (middle + (mlp_own + mlp_peer) + back_bias).astype(bf16)
+        dq, dk, dv, qv_sums = attend_back(q, k, v, do, lse_a, lse_b, ids_col, ids_row)
+        qkv_parts = [weight_grad(parts, exchange.place, normed, a) for a in (dq, dk, dv)]
+        dn1 = normed_back(dq, dk, dv, w3)
+        dn1_peer = other_core(dn1)
+        tokens_grad, input_sums = input_back(tokens, dn1, dn1_peer, dh, row(norm1_gain))
+
+        w_back_grad = jnp.transpose(exchange.reduce(back_parts))
+        w_in_grad = exchange.reduce(in_parts)
+        w_out_grad = jnp.transpose(exchange.reduce(out_parts))
+        w_qkv_grad = jnp.stack([exchange.reduce(p) for p in qkv_parts], 1)
+
+        pieces = [input_sums[0], input_sums[1], middle_sums[2], middle_sums[0], middle_sums[1], back_bias_sum[0]]
+        pieces += [qv_sums[0], qv_sums[1], in_bias_sum[0]]
+        packed = jnp.concatenate([p.reshape(batch, -1) for p in pieces], 1)
+        vectors = lax.psum_scatter(packed, "batch", scatter_dimension=0, tiled=True)[0]
     out, at = [], 0
     for p in pieces:
         n = p.shape[0] // batch

time: 385 us -> 220 us (0.57)
  waiting for transfers between devices: 84.5 us -> 0.01 us
  Pallas kernels: 114 us -> 194 us
  blocking collectives: 74.2 us -> 0 us
  starting transfers between devices: 42.7 us -> 0.62 us
  local copies, waits for them, and re-layouts: 47.3 us -> 23.6 us
  other arithmetic: 20.2 us -> 0.57 us
    ppermute x30 -> x0, waiting for transfers between devices: 84.4 us -> none  [swap(): return lax.ppermute(block, ('batch', 'tp'), perm)]
    unnamed x1 -> x0, blocking collectives: 74.2 us -> none
    pallas_call x12 -> x1, Pallas kernels: 74.4 us -> 148 us  [tail(): pl.pallas_call(tail_kernel, in_specs=[hbm] * 15 + [vmem] * 7, out_specs=[...]
    ppermute x30 -> x0, starting transfers between devices: 41.6 us -> none  [swap(): return lax.ppermute(block, ('batch', 'tp'), perm)]
    unnamed x127 -> x19, local copies, waits for them, and re-layouts: 39.5 us -> 5.77 us
    add x13 -> x0, other arithmetic: 10.6 us -> none  [the longest x12 8.55 us: reduce(): total = total + cut(g, i)]
    convert_element_type x1 -> x0, other arithmetic: 5.45 us -> none  [shards(): layer_out = (middle + (mlp_own + mlp_peer) + back_bias).astype(bf16)]
    reshape x6 -> x7, local copies, waits for them, and re-layouts: 1.4 us -> 5.5 us  [shards(): row = lambda a: a.reshape(1, -1)]
  transfers between devices with their start and end apart: 35 -> 2, of which waited for: 14 -> 0; matrix products, arithmetic and copies ran while one was open for 6% -> 1% of each run, Pallas kernels for 21% -> 9%
where the time goes in v2:
time: 220 us
  Pallas kernels  194 us (88%)
  local copies, waits for them, and re-layouts  23.6 us (11%)
    pallas_call x1, Pallas kernels, tail(): pl.pallas_call(tail_kernel, in_specs=[hbm] * 15 + [vmem] * 7, out_specs=[...  148 us
    pallas_call x2, Pallas kernels, attend(): pl.pallas_call(functools.partial(attend_kernel, half), grid=(width // PAI...  24 us
    pallas_call x2, Pallas kernels, hidden_layer(): pl.pallas_call(hidden_kernel, grid=(per,), in_specs=[glob(dim), loc(dim),...  15.5 us
    pallas_call x1, Pallas kernels, project(): pl.pallas_call(project_kernel, grid=(tok // TILE,), in_specs=[rows(dim),...  7 us
    unnamed x19, local copies, waits for them, and re-layouts  5.77 us
    reshape x7, local copies, waits for them, and re-layouts, shards(): row = lambda a: a.reshape(1, -1)  5.5 us
  transfers between devices with their start and end apart: 2, of which 0 were waited for; matrix products, arithmetic and copies ran while one was open for 1% of the time, Pallas kernels for 9%

profile of v2, /device:TPU:0, one launch (start us, length us, event | category | flops | bytes accessed | tf_op | source)
XLA Modules:
  0.0 219.7 jit_solution(8644290031969998780)
XLA Ops:
  0.6 1.8 reshape.89.col_ref
  2.4 1.3 reshape.80.row_ref
  3.7 1.3 reshape.77.gain_ref.gain1_ref
  5.0 1.3 reshape.78.shift_ref
  6.2 7.0 %project.1 = (bf16[1216,768]{1,0:T(8,128)(2,1)}, bf16[1216,384]{1,0:T(8,128)(2,1)}, bf16[1216,384]{1,0:T(8,128)(2,1)}, bf16[1216,384]{1,0:T(8,128)(2,1)}) custom-call(bf16[1216,768]{1,0:T(8,128)(2,1)} %tok_h.1, f32[1,768]{1,0:T(1,128)} %reshape.77.gain_ref.gain1_ref, f32[1,768]{1,0:T(1,128)} %reshape.78.shift_ref, bf16[3,768,384]{2,1,0:T(8,128)(2,1)} %bitcast.31, ...), custom_call_target="tpu_custom_call" | custom-call | flops 2151677952 | bytes 8306688 | tf_op jit(solution)/shard_map/project/pallas_call | solution.py:76
  13.2 11.7 %attend.2 = (bf16[1216,384]{1,0:T(8,128)(2,1)}, f32[2,8,384]{2,1,0:T(8,128)}, f32[608,768]{1,0:T(8,128)}) custom-call(bf16[1216,384]{1,0:T(8,128)(2,1)} %get-tuple-element.36.q_ref.q_h, bf16[1216,384]{1,0:T(8,128)(2,1)} %get-tuple-element.37.k_ref.k_h, bf16[1216,384]{1,0:T(8,128)(2,1)} %get-tuple-element.38.v_ref.v_h, s32[1216,1]{1,0:T(8,128)} %reshape.89.col_ref, ...), custom_call_target="tpu_custom_call" | custom-call | flops 2428108800 | bytes 4669440 | tf_op jit(solution)/shard_map/attend/pallas_call | solution.py:142
  25.5 12.3 %attend.3 = (bf16[1216,384]{1,0:T(8,128)(2,1)}, f32[2,8,384]{2,1,0:T(8,128)}, f32[608,768]{1,0:T(8,128)}) custom-call(bf16[1216,384]{1,0:T(8,128)(2,1)} %get-tuple-element.36.q_ref.q_h, bf16[1216,384]{1,0:T(8,128)(2,1)} %get-tuple-element.37.k_ref.k_h, bf16[1216,384]{1,0:T(8,128)(2,1)} %get-tuple-element.38.v_ref.v_h, ...), custom_call_target="tpu_custom_call", output_to_operand_aliasing={{0}: (6, {})} | custom-call | flops 2428108800 | bytes 4669440 | tf_op jit(solution)/shard_map/attend/pallas_call | solution.py:142
  38.5 0.6 reshape.84.ib_ref
  40.9 7.8 %hidden_layer.2 = (f32[1216,768]{1,0:T(8,128)}, bf16[1216,768]{1,0:T(8,128)(2,1)}, bf16[1216,1536]{1,0:T(8,128)(2,1)}, bf16[1216,1536]{1,0:T(8,128)(2,1)}) custom-call(bf16[1216,768]{1,0:T(8,128)(2,1)} %tok_h.1, f32[608,768]{1,0:T(8,128)} %get-tuple-element.41.own_ref, f32[608,768]{1,0:T(8,128)} %collective-permute-done.1.peer_ref, ...), custom_call_target="tpu_custom_call" | custom-call | flops 1434451968 | bytes 13565952 | tf_op jit(solution)/shard_map/hidden_layer/pallas_call | solution.py:194
  48.7 1.2 copy-done
  49.9 7.7 %hidden_layer.3 = (f32[1216,768]{1,0:T(8,128)}, bf16[1216,768]{1,0:T(8,128)(2,1)}, bf16[1216,1536]{1,0:T(8,128)(2,1)}, bf16[1216,1536]{1,0:T(8,128)(2,1)}) custom-call(bf16[1216,768]{1,0:T(8,128)(2,1)} %tok_h.1, f32[608,768]{1,0:T(8,128)} %get-tuple-element.40.own_ref, ...), custom_call_target="tpu_custom_call", output_to_operand_aliasing={{0}: (8, {}), {1}: (9, {}), {2}: (10, {}), {3}: (11, {})} | custom-call | flops 1434451968 | bytes 13565952 | tf_op jit(solution)/shard_map/hidden_layer/pallas_call | solution.py:194
  57.6 147.7 %tail.1 = (bf16[1216,768]{1,0:T(8,128)(2,1)}, bf16[1216,768]{1,0:T(8,128)(2,1)}, f32[12,48,384]{2,1,0:T(8,128)}, f32[8,1536]{1,0:T(8,128)}) custom-call(bf16[1216,768]{1,0:T(8,128)(2,1)} %g_h.1, bf16[1216,1536]{1,0:T(8,128)(2,1)} %get-tuple-element.46.hid_h, bf16[1216,1536]{1,0:T(8,128)(2,1)} %get-tuple-element.47.slope_h, ...), custom_call_target="tpu_custom_call" | custom-call | flops 24000000000 | bytes 40000000 | tf_op jit(solution)/shard_map/tail/pallas_call | solution.py:938
  205.3 1.0 slice_reduce_fusion.1
  206.3 0.8 slice_reduce_fusion
  207.1 0.7 slice_reduce_fusion.7
  207.9 1.1 slice_bitcast_fusion
  209.0 1.6 slice_bitcast_fusion.2
  210.6 1.5 slice_bitcast_fusion.3
  212.8 0.7 copy.39
  213.6 0.7 copy.40
  215.7 0.6 dynamic-slice_bitcast_fusion
  216.3 1.2 copy.48
  217.5 0.9 copy-done.1
  218.4 1.2 copy.49
  (35 shorter events, 5.0 us)
Async XLA Ops:
  25.0 15.9 %collective-permute-start.1 = (f32[608,768]{1,0:T(8,128)}, f32[608,768]{1,0:T(8,128)}, u32[]{:S(2)}, u32[]{:S(2)}) collective-permute-start(f32[608,768]{1,0:T(8,128)} %get-tuple-element.41.own_ref), channel_id=1, source_target_pairs={{0,1},{1,0},{2,3},{3,2},{4,5},{5,4},{6,7},{7,6},{8,9},{9,8},{10,11... | collective-permute-start | bytes 5603336 | tf_op jit(solution)/shard_map/ppermute | solution.py:556
  25.5 12.4 %copy-start.4 = (f32[768]{0:T(1024)S(1)}, f32[768]{0:T(1024)}, u32[]{:S(2)}) copy-start(f32[768]{0:T(1024)} %param.24) | copy-start | bytes 9220
  25.5 13.0 %copy-start.3 = (f32[1536]{0:T(1024)S(1)}, f32[1536]{0:T(1024)}, u32[]{:S(2)}) copy-start(f32[1536]{0:T(1024)} %param.27) | copy-start | bytes 18436
  25.5 13.6 %copy-start.5 = (f32[768]{0:T(1024)S(1)}, f32[768]{0:T(1024)}, u32[]{:S(2)}) copy-start(f32[768]{0:T(1024)} %param.23) | copy-start | bytes 9220
  25.5 14.2 %copy-start.6 = (f32[768]{0:T(1024)S(1)}, f32[768]{0:T(1024)}, u32[]{:S(2)}) copy-start(f32[768]{0:T(1024)} %param.25) | copy-start | bytes 9220
  25.5 14.8 %copy-start.7 = (f32[768]{0:T(1024)S(1)}, f32[768]{0:T(1024)}, u32[]{:S(2)}) copy-start(f32[768]{0:T(1024)} %param.29) | copy-start | bytes 9220
  37.8 10.9 %collective-permute-start = (f32[608,768]{1,0:T(8,128)}, f32[608,768]{1,0:T(8,128)S(1)}, u32[]{:S(2)}, u32[]{:S(2)}) collective-permute-start(f32[608,768]{1,0:T(8,128)} %get-tuple-element.40.own_ref), channel_id=1, source_target_pairs={{0,1},{1,0},{2,3},{3,2},{4,5},{5,4},{6,7},{7,6},{8,9},{9,8},{10,11... | collective-permute-start | bytes 5603336 | tf_op jit(solution)/shard_map/ppermute | solution.py:556
  48.7 1.2 copy-start
  205.3 11.0 %copy-start.2 = (bf16[1216,768]{1,0:T(8,128)(2,1)S(1)}, bf16[1216,768]{1,0:T(8,128)(2,1)}, u32[]{:S(2)}) copy-start(bf16[1216,768]{1,0:T(8,128)(2,1)} %get-tuple-element.90) | copy-start | bytes 5603332
  216.3 2.2 copy-start.1
